TPU v7x, 512 devices: a whole 4x8x8 slice. The times are simulated.
512 devices in a mesh: dx: 128 (over y, z_hi, x), dy: 4 (over z_lo, core).
Axes of the slice: x: 4, y: 8, z: 8 (z_hi: 4, z_lo: 2; z = z_hi * 2 + z_lo), core: 2. Of those that a mesh axis runs over, the one named last changes fastest.
Arguments:
- features: bfloat16 [65536, 128], P(('dx', 'dy')), may hold values from -6 to 6
- positions: float32 [3, 65536], P(None, ('dx', 'dy')), may hold values from 0 to 1, as said below
- neighbours: int32 [65536, 64], P(('dx', 'dy')), may hold values from 0 to 256, as said below
- distances: float32 [65536, 64], P(('dx', 'dy')), may hold values from 0.5 to 5
- ghost_rows: int32 [4, 16384], P(None, ('dx', 'dy')), may hold values from 0 to 127, as said below
- atom_counts: int32 [512], P(('dx', 'dy')), may hold values from 64 to 128, as said below
- wavevectors: float32 [3, 2048], replicated, may hold values from -40 to 40
- wave_weights: float32 [2048], replicated, may hold values from 0.05 to 1
- source_weight: bfloat16 [128, 128], replicated, may hold values from -0.5 to 0.5
- target_weight: bfloat16 [128, 128], replicated, may hold values from -0.5 to 0.5
- edge_weight: bfloat16 [128, 128], replicated, may hold values from -0.5 to 0.5
- mix_weight: bfloat16 [128, 128], replicated, may hold values from -0.0625 to 0.0625
- charge_weight: bfloat16 [128, 64], replicated, may hold values from -0.5 to 0.5
- field_weight: bfloat16 [64, 128], replicated, may hold values from -0.75 to 0.75
- cotangent: bfloat16 [65536, 128], P(('dx', 'dy')), may hold values from -6 to 6
Outputs:
- layer_output: bfloat16 [65536, 128], P(('dx', 'dy'))
- feature_grad: bfloat16 [65536, 128], P(('dx', 'dy'))
- source_grad: float32 [128, 128], replicated
- target_grad: float32 [128, 128], replicated
- edge_grad: float32 [128, 128], replicated
- mix_grad: float32 [128, 128], replicated
- charge_grad: float32 [128, 64], replicated
- field_grad: float32 [64, 128], replicated
Inputs may be any that keep to these rules, and one draw needn't show every extreme that they name: `atom_counts`: each domain's count of live atoms; slots from that count on are padding. Some domain is full and some holds exactly half of 128. `neighbours`: an entry below 128 names a live atom of the row's own domain; 128 + f * 32 + g names ghost row g of block f of the domain's table; 256 marks an empty slot. `ghost_rows`: column block d of row f lists live atoms of domain d that it sends over face f (f = 0: to the domain after it along dx, 1: before it along dx, 2: after it along dy, 3: before it along dy, with wrap); rows may repeat. `positions`: each atom lies in its domain's part of the unit box: its first coordinate within [ix / 128, (ix + 1) / 128) and its second within [iy / 4, (iy + 1) / 4) for the domain's indices ix, iy.
All inputs are finite; a program needn't handle non-finite values.
Results may differ from a plain program's by a relative error of at most 0.011.
Values may be sent and summed in bfloat16 or wider, within the bound.
A program may use at most 64 MiB of HBM per device.

v0:
```python
import math

import jax
import jax.numpy as jnp
from jax import lax
from jax.sharding import PartitionSpec as P

K = 2048


cutoff_rate = math.pi / 5.0


def passed_along(block, axis, distance):
    devices = range(lax.axis_size(axis))
    route = [((i - distance) % len(devices), i) for i in devices]
    return lax.ppermute(block, axis, route)


def silu_slope(argument):
    logistic = jax.nn.sigmoid(argument)
    return logistic * (1.0 + argument * (1.0 - logistic))


def contract_rows(left_side, right_side):
    return lax.dot_general(
        left_side, right_side, (((0,), (0,)), ((), ())), preferred_element_type=jnp.float32
    )


def contract_cols(left_side, right_side):
    return lax.dot_general(
        left_side, right_side, (((1,), (1,)), ((), ())), preferred_element_type=jnp.float32
    )


def phases(coords, wave_table):
    phase_angle = (
        coords[0][:, None] * wave_table[0][None, :]
        + coords[1][:, None] * wave_table[1][None, :]
        + coords[2][:, None] * wave_table[2][None, :]
    )
    return (jnp.cos(phase_angle).astype(jnp.bfloat16), jnp.sin(phase_angle).astype(jnp.bfloat16))


def weigh_totals(totals, factor):
    return (totals * factor[:, None]).astype(jnp.bfloat16)


def along_x(payload, offset):
    return passed_along(payload, "dx", offset)


def along_y(payload, offset):
    return passed_along(payload, "dy", offset)


def edge_geometry(source, target_table, neighbour, distance):
    nearby = target_table[neighbour]
    summed = source[:, None, :].astype(jnp.float32) + nearby.astype(jnp.float32)
    validity = (neighbour < target_table.shape[0] - 1).astype(jnp.float32)
    edge_gate = validity * (0.5 + 0.5 * jnp.cos(distance * cutoff_rate))
    return (summed, edge_gate)


def edge_forward(source, target_table, neighbour, distance, edge_weight):
    summed, edge_gate = edge_geometry(source, target_table, neighbour, distance)
    hidden = jax.nn.silu(summed).astype(jnp.bfloat16)
    row_total = hidden.shape[0] * hidden.shape[1]
    mixed = jnp.dot(
        hidden.reshape(row_total, hidden.shape[2]), edge_weight, preferred_element_type=jnp.float32
    )
    message = jax.nn.silu(mixed).reshape(summed.shape)
    return jnp.sum(edge_gate[:, :, None] * message, axis=1).astype(jnp.bfloat16)


def edge_backward(source, target_table, neighbour, distance, edge_weight, upstream):
    summed, edge_gate = edge_geometry(source, target_table, neighbour, distance)
    hidden = jax.nn.silu(summed).astype(jnp.bfloat16)
    row_total = hidden.shape[0] * hidden.shape[1]
    hidden_flat = hidden.reshape(row_total, hidden.shape[2])
    mixed = jnp.dot(hidden_flat, edge_weight, preferred_element_type=jnp.float32)
    slopes = silu_slope(mixed).reshape(summed.shape)
    inner_grad = (edge_gate[:, :, None] * upstream[:, None, :].astype(jnp.float32) * slopes).astype(
        jnp.bfloat16
    )
    inner_flat = inner_grad.reshape(row_total, inner_grad.shape[2])
    edge_part = contract_rows(hidden_flat, inner_flat)
    outer_grad = contract_cols(inner_flat, edge_weight).reshape(summed.shape)
    pair_grad = (outer_grad * silu_slope(summed)).astype(jnp.bfloat16)
    source_part = jnp.sum(pair_grad.astype(jnp.float32), axis=1)
    table_part = (
        jnp.zeros((target_table.shape[0], pair_grad.shape[2]), jnp.float32)
        .at[neighbour.reshape(-1)]
        .add(pair_grad.reshape(row_total, pair_grad.shape[2]).astype(jnp.float32))
    )
    return (edge_part, source_part, table_part)


def local(
    features,
    positions,
    neighbours,
    distances,
    ghost_rows,
    atom_counts,
    wavevectors,
    wave_weights,
    source_weight,
    target_weight,
    edge_weight,
    mix_weight,
    charge_weight,
    field_weight,
    cotangent,
):
    atom_slots = features.shape[0]
    channels = features.shape[1]
    ghosts = ghost_rows.shape[1]
    total_atoms = atom_slots * lax.axis_size("dx") * lax.axis_size("dy")
    factor = wave_weights * (4.0 / math.sqrt(total_atoms * K))
    alive_mask = (jnp.arange(atom_slots, dtype=jnp.int32) < atom_counts[0]).astype(jnp.bfloat16)
    masked = features * alive_mask[:, None]
    source = jnp.dot(masked, source_weight, preferred_element_type=jnp.float32).astype(jnp.bfloat16)
    target = jnp.dot(masked, target_weight, preferred_element_type=jnp.float32).astype(jnp.bfloat16)
    charge = jnp.dot(masked, charge_weight, preferred_element_type=jnp.float32).astype(jnp.bfloat16)
    grad_masked = cotangent * alive_mask[:, None]
    grad_aggregate = contract_cols(grad_masked, mix_weight).astype(jnp.bfloat16)
    grad_potential = contract_cols(grad_masked, field_weight).astype(jnp.bfloat16)
    cosine_rows, sine_rows = phases(positions, wavevectors)

    def long_range(values):
        partial_cos = contract_rows(cosine_rows, values)
        partial_sin = contract_rows(sine_rows, values)
        total_cos, total_sin = lax.psum((partial_cos, partial_sin), ("dx", "dy"))
        weight_cos = weigh_totals(total_cos, factor)
        weight_sin = weigh_totals(total_sin, factor)
        return (
            jnp.dot(cosine_rows, weight_cos, preferred_element_type=jnp.float32)
            + jnp.dot(sine_rows, weight_sin, preferred_element_type=jnp.float32)
        ).astype(jnp.bfloat16)

    potential = long_range(charge)
    outgoing = target[ghost_rows]
    incoming = jnp.concatenate(
        [
            along_x(outgoing[0], 1),
            along_x(outgoing[1], -1),
            along_y(outgoing[2], 1),
            along_y(outgoing[3], -1),
        ],
        axis=0,
    )
    target_table = jnp.concatenate(
        [target, incoming, jnp.zeros((1, channels), jnp.bfloat16)], axis=0
    )
    block_size = min(64, atom_slots)
    block_count = atom_slots // block_size

    def split_rows(array):
        return array.reshape((block_count, block_size) + array.shape[1:])

    def forward_block(block_items):
        return edge_forward(
            block_items[0], target_table, block_items[1], block_items[2], edge_weight
        )

    aggregate = lax.map(
        forward_block, (split_rows(source), split_rows(neighbours), split_rows(distances))
    ).reshape(atom_slots, channels)
    alive_wide = alive_mask.astype(jnp.float32)[:, None]
    layer_output = (
        alive_wide
        * (
            jnp.dot(aggregate, mix_weight, preferred_element_type=jnp.float32)
            + jnp.dot(potential, field_weight, preferred_element_type=jnp.float32)
        )
    ).astype(jnp.bfloat16)
    grad_charge = long_range(grad_potential)

    def backward_block(running, block_items):
        edge_part, source_part, table_part = edge_backward(
            block_items[0],
            target_table,
            block_items[1],
            block_items[2],
            edge_weight,
            block_items[3],
        )
        return ((running[0] + edge_part, running[1] + table_part), source_part)

    zero_edge = jnp.zeros((channels, channels), jnp.float32)
    zero_table = jnp.zeros((target_table.shape[0], channels), jnp.float32)
    sums, source_blocks = lax.scan(
        backward_block,
        (zero_edge, zero_table),
        (
            split_rows(source),
            split_rows(neighbours),
            split_rows(distances),
            split_rows(grad_aggregate),
        ),
    )
    edge_sum, table_sum = sums
    grad_source = source_blocks.reshape(atom_slots, channels).astype(jnp.bfloat16)
    ghost_grad = (
        table_sum[atom_slots : atom_slots + 4 * ghosts]
        .astype(jnp.bfloat16)
        .reshape(4, ghosts, channels)
    )
    returned = jnp.concatenate(
        [
            along_x(ghost_grad[0], -1),
            along_x(ghost_grad[1], 1),
            along_y(ghost_grad[2], -1),
            along_y(ghost_grad[3], 1),
        ],
        axis=0,
    ).astype(jnp.float32)
    target_sum = table_sum[:atom_slots].at[ghost_rows.reshape(-1)].add(returned)
    grad_target = target_sum.astype(jnp.bfloat16)
    feature_grad = (
        alive_wide
        * (
            contract_cols(grad_source, source_weight)
            + contract_cols(grad_target, target_weight)
            + contract_cols(grad_charge, charge_weight)
        )
    ).astype(jnp.bfloat16)
    weight_grads = lax.psum(
        (
            contract_rows(masked, grad_source),
            contract_rows(masked, grad_target),
            edge_sum,
            contract_rows(aggregate, grad_masked),
            contract_rows(masked, grad_charge),
            contract_rows(potential, grad_masked),
        ),
        ("dx", "dy"),
    )
    grad_scale = 1.0 / math.sqrt(total_atoms)
    return (
        layer_output,
        feature_grad,
        weight_grads[0] * grad_scale,
        weight_grads[1] * grad_scale,
        weight_grads[2] * grad_scale,
        weight_grads[3] * grad_scale,
        weight_grads[4] * grad_scale,
        weight_grads[5] * grad_scale,
    )


def solution(mesh):
    in_specs = (
        P(("dx", "dy"), None),
        P(None, ("dx", "dy")),
        P(("dx", "dy"), None),
        P(("dx", "dy"), None),
        P(None, ("dx", "dy")),
        P(("dx", "dy")),
        P(),
        P(),
        P(),
        P(),
        P(),
        P(),
        P(),
        P(),
        P(("dx", "dy"), None),
    )
    out_specs = (P(("dx", "dy"), None), P(("dx", "dy"), None), P(), P(), P(), P(), P(), P())
    return jax.shard_map(local, mesh=mesh, in_specs=in_specs, out_specs=out_specs, check_vma=False)
```

profile of v0, /device:TPU:1, one launch (start us, length us, event | category | flops | bytes accessed | tf_op | source)
XLA Modules:
  0.0 773.1 jit_solution(8975965893310532262)
XLA Ops:
  10.4 3.9 collective-permute-start
  14.3 14.6 %collective-permute-start.1 = (bf16[32,128]{1,0:T(8,128)(2,1)S(1)}, bf16[32,128]{1,0:T(8,128)(2,1)S(1)}, u32[]{:S(2)}, u32[]{:S(2)}) collective-permute-start(bf16[32,128]{1,0:T(8,128)(2,1)S(1)} %get-tuple-element.197), channel_id=1, source_target_pairs={{4,0},{8,4},{12,8},{16,12},{20,16},{24,20},{28,24},{32,28},{36,32}... | collective-permute-start | bytes 24584 | tf_op jit(solution)/shard_map/ppermute | solution.py:17
  28.9 3.9 collective-permute-start.2
  38.2 4.8 fusion.52
  43.0 4.8 fusion.54
  48.1 4.8 fusion.53
  52.9 5.1 fusion.55
  59.3 94.0 %while.26 = (s32[]{:T(128)}, f32[128,128]{1,0:T(8,128)}, f32[257,128]{1,0:T(8,128)S(1)}, bf16[2,64,128]{2,1,0:T(8,128)(2,1)}, bf16[2,64,128]{2,1,0:T(8,128)(2,1)...) while((s32[]{:T(128)}, f32[128,128]{1,0:T(8,128)}, ...), condition=%wide.region_8.9_spmd.clone, body=%wide.region_5.8_spmd.clone.sunk | while | flops 424239104 | bytes 28296096 | solution.py:194
  59.6 12.1 %gather_fusion.1 = bf16[4096,128]{1,0:T(8,128)(2,1)S(1)} fusion(bf16[257,128]{1,0:T(8,128)(2,1)S(1)} %get-tuple-element.382, s32[4096]{0:T(1024)S(1)} %broadcast_clamp_fusion.5), kind=kCustom, calls=%fused_computation.1.clone.clone.1 | custom fusion | bytes 2113536 | tf_op jit(solution)/shard_map/while/body/eval_jaxpr/gather | solution.py:59
  79.1 22.5 %scatter_fusion = f32[257,128]{1,0:T(8,128)S(1)} fusion(f32[257,128]{1,0:T(8,128)S(1)} %get-tuple-element.366, s32[4096]{0:T(1024)} %bitcast.184, f32[4096,128]{1,0:T(8,128)S(1)} %bitcast.178), kind=kCustom, calls=%fused_computation.3.clone.clone.1 | custom fusion | flops 524288 | bytes 6307840 | tf_op jit(solution)/shard_map/while/body/eval_jaxpr/scatter-add | solution.py:95
  103.0 3.3 fusion.109
  106.6 12.1 %gather_fusion.1 = bf16[4096,128]{1,0:T(8,128)(2,1)S(1)} fusion(bf16[257,128]{1,0:T(8,128)(2,1)S(1)} %get-tuple-element.382, s32[4096]{0:T(1024)S(1)} %broadcast_clamp_fusion.5), kind=kCustom, calls=%fused_computation.1.clone.clone.1 | custom fusion | bytes 2113536 | tf_op jit(solution)/shard_map/while/body/eval_jaxpr/gather | solution.py:59
  126.1 22.5 %scatter_fusion = f32[257,128]{1,0:T(8,128)S(1)} fusion(f32[257,128]{1,0:T(8,128)S(1)} %get-tuple-element.366, s32[4096]{0:T(1024)} %bitcast.184, f32[4096,128]{1,0:T(8,128)S(1)} %bitcast.178), kind=kCustom, calls=%fused_computation.3.clone.clone.1 | custom fusion | flops 524288 | bytes 6307840 | tf_op jit(solution)/shard_map/while/body/eval_jaxpr/scatter-add | solution.py:95
  150.0 3.3 fusion.109
  153.4 3.6 collective-permute-start.4
  166.5 29.8 %while.25 = (s32[]{:T(128)}, bf16[2,64,128]{2,1,0:T(8,128)(2,1)}, s32[2,64,64]{2,1,0:T(8,128)S(1)}, f32[2,64,64]{2,1,0:T(8,128)S(1)}, bf16[2,64,128]{2,1,0:T(8,1...) while((s32[]{:T(128)}, bf16[2,64,128]{2,1,0:T(8,128)(2,1)}, ...), condition=%wide.region_2.3_spmd, body=%wide.region_0.2_spmd.sunk | while | flops 141070336 | bytes 10043549 | solution.py:168
  166.6 12.1 %gather_fusion = bf16[4096,128]{1,0:T(8,128)(2,1)S(1)} fusion(bf16[257,128]{1,0:T(8,128)(2,1)S(1)} %get-tuple-element.349, s32[4096]{0:T(1024)S(1)} %broadcast_clamp_fusion.4), kind=kCustom, calls=%fused_computation.clone.1 | custom fusion | bytes 2113536 | tf_op jit(solution)/shard_map/while/body/eval_jaxpr/gather | solution.py:59
  181.5 12.1 %gather_fusion = bf16[4096,128]{1,0:T(8,128)(2,1)S(1)} fusion(bf16[257,128]{1,0:T(8,128)(2,1)S(1)} %get-tuple-element.349, s32[4096]{0:T(1024)S(1)} %broadcast_clamp_fusion.4), kind=kCustom, calls=%fused_computation.clone.1 | custom fusion | bytes 2113536 | tf_op jit(solution)/shard_map/while/body/eval_jaxpr/gather | solution.py:59
  201.5 284.5 %all-reduce.7.cloned.1.call-done = (f32[2048,64]{1,0:T(8,128)}, f32[2048,64]{1,0:T(8,128)}, f32[2048,64]{1,0:T(8,128)}, f32[2048,64]{1,0:T(8,128)}, f32[128,128]...) async-done(((f32[2048,64]{1,0:T(8,128)}, f32[2048,64]{1,0:T(8,128)}, f32[2048,64]{1,0:T(8,128)}, f32[2048,64]{1,0:T(8,128)}, ...) | async-done | bytes 2359312 | tf_op jit(solution)/shard_map/psum | solution.py:135
  486.0 5.1 fusion.23
  491.1 5.1 fusion.21
  497.1 3.8 fusion.22
  500.9 4.0 fusion.20
  508.8 254.5 %all-reduce.5.cloned.1.call-done = (f32[128,64]{0,1:T(8,128)}, f32[64,128]{1,0:T(8,128)}) async-done(((f32[128,64]{0,1:T(8,128)}, f32[64,128]{1,0:T(8,128)}), (f32[128,64]{0,1:T(8,128)}, f32[64,128]{1,0:T(8,128)})) %all-reduce.5.cloned.1.call-update) | async-done | bytes 65552 | tf_op jit(solution)/shard_map/psum | solution.py:230
  (226 shorter events, 54.5 us)
Async XLA Ops:
  7.2 40.6 %copy-start.18 = (bf16[128,128]{1,0:T(8,128)(2,1)S(1)}, bf16[128,128]{1,0:T(8,128)(2,1)}, u32[]{:S(2)}) copy-start(bf16[128,128]{1,0:T(8,128)(2,1)} %param.19) | copy-start | bytes 98308
  7.2 40.6 %copy-start.28 = (bf16[128,64]{0,1:T(8,128)(2,1)S(1)}, bf16[128,64]{0,1:T(8,128)(2,1)}, u32[]{:S(2)}) copy-start(bf16[128,64]{0,1:T(8,128)(2,1)} %param.31) | copy-start | bytes 49156
  7.2 478.8 %all-reduce.7.cloned.1.call-start = ((), (), s32[]{:S(2)}) async-start(), calls=%async_computation.1 | async-start | bytes 8912896 | tf_op jit(solution)/shard_map/psum | solution.py:135
  7.9 50.3 %copy-start.36 = (bf16[128]{0:T(256)(128)(2,1)}, bf16[128]{0:T(256)(128)(2,1)S(1)}, u32[]{:S(2)}) copy-start(bf16[128]{0:T(256)(128)(2,1)S(1)} %compare_convert_fusion) | copy-start | bytes 772
  10.4 48.8 %collective-permute-start = (bf16[32,128]{1,0:T(8,128)(2,1)S(1)}, bf16[32,128]{1,0:T(8,128)(2,1)S(1)}, u32[]{:S(2)}, u32[]{:S(2)}) collective-permute-start(bf16[32,128]{1,0:T(8,128)(2,1)S(1)} %get-tuple-element.198), channel_id=1, source_target_pairs={{508,0},{0,4},{4,8},{8,12},{12,16},{16,20},{20,24},{24,28},{28,32}... | collective-permute-start | bytes 24584 | tf_op jit(solution)/shard_map/ppermute | solution.py:17
  14.3 44.8 %collective-permute-start.1 = (bf16[32,128]{1,0:T(8,128)(2,1)S(1)}, bf16[32,128]{1,0:T(8,128)(2,1)S(1)}, u32[]{:S(2)}, u32[]{:S(2)}) collective-permute-start(bf16[32,128]{1,0:T(8,128)(2,1)S(1)} %get-tuple-element.197), channel_id=1, source_target_pairs={{4,0},{8,4},{12,8},{16,12},{20,16},{24,20},{28,24},{32,28},{36,32}... | collective-permute-start | bytes 24584 | tf_op jit(solution)/shard_map/ppermute | solution.py:17
  28.9 30.3 %collective-permute-start.2 = (bf16[32,128]{1,0:T(8,128)(2,1)S(1)}, bf16[32,128]{1,0:T(8,128)(2,1)S(1)}, u32[]{:S(2)}, u32[]{:S(2)}) collective-permute-start(bf16[32,128]{1,0:T(8,128)(2,1)S(1)} %get-tuple-element.196), channel_id=1, source_target_pairs={{3,0},{0,1},{1,2},{2,3},{7,4},{4,5},{5,6},{6,7},{11,8},{8,9},{9,10... | collective-permute-start | bytes 24584 | tf_op jit(solution)/shard_map/ppermute | solution.py:17
  32.9 26.4 %collective-permute-start.3 = (bf16[32,128]{1,0:T(8,128)(2,1)S(1)}, bf16[32,128]{1,0:T(8,128)(2,1)S(1)}, u32[]{:S(2)}, u32[]{:S(2)}) collective-permute-start(bf16[32,128]{1,0:T(8,128)(2,1)S(1)} %get-tuple-element.195), channel_id=1, source_target_pairs={{1,0},{2,1},{3,2},{0,3},{5,4},{6,5},{7,6},{4,7},{9,8},{10,9},{11,1... | collective-permute-start | bytes 24584 | tf_op jit(solution)/shard_map/ppermute | solution.py:17
  36.4 16.4 %copy-start.32 = (f32[1,2048]{1,0:T(1,128)}, f32[1,2048]{1,0:T(1,128)S(1)}, u32[]{:S(2)}) copy-start(f32[1,2048]{1,0:T(1,128)S(1)} %get-tuple-element.193) | copy-start | bytes 24580
  79.1 23.8 %copy-start.4 = (f32[64,128]{1,0:T(8,128)S(1)}, f32[64,128]{1,0:T(8,128)}, u32[]{:S(2)}) copy-start(f32[64,128]{1,0:T(8,128)} %copy-done.2) | copy-start | bytes 98308 | tf_op jit(solution)/shard_map/while
  126.1 23.8 %copy-start.4 = (f32[64,128]{1,0:T(8,128)S(1)}, f32[64,128]{1,0:T(8,128)}, u32[]{:S(2)}) copy-start(f32[64,128]{1,0:T(8,128)} %copy-done.2) | copy-start | bytes 98308 | tf_op jit(solution)/shard_map/while
  153.4 44.6 %collective-permute-start.4 = (bf16[32,128]{1,0:T(8,128)(2,1)S(1)}, bf16[32,128]{1,0:T(8,128)(2,1)S(1)}, u32[]{:S(2)}, u32[]{:S(2)}) collective-permute-start(bf16[32,128]{1,0:T(8,128)(2,1)S(1)} %get-tuple-element.188), channel_id=1, source_target_pairs={{4,0},{8,4},{12,8},{16,12},{20,16},{24,20},{28,24},{32,28},{36,32}... | collective-permute-start | bytes 24584 | tf_op jit(solution)/shard_map/ppermute | solution.py:17
  157.0 40.9 %collective-permute-start.5 = (bf16[32,128]{1,0:T(8,128)(2,1)S(1)}, bf16[32,128]{1,0:T(8,128)(2,1)S(1)}, u32[]{:S(2)}, u32[]{:S(2)}) collective-permute-start(bf16[32,128]{1,0:T(8,128)(2,1)S(1)} %get-tuple-element.191), channel_id=1, source_target_pairs={{508,0},{0,4},{4,8},{8,12},{12,16},{16,20},{20,24},{24,28},{28,32}... | collective-permute-start | bytes 24584 | tf_op jit(solution)/shard_map/ppermute | solution.py:17
  158.9 39.0 %collective-permute-start.6 = (bf16[32,128]{1,0:T(8,128)(2,1)S(1)}, bf16[32,128]{1,0:T(8,128)(2,1)S(1)}, u32[]{:S(2)}, u32[]{:S(2)}) collective-permute-start(bf16[32,128]{1,0:T(8,128)(2,1)S(1)} %get-tuple-element.190), channel_id=1, source_target_pairs={{1,0},{2,1},{3,2},{0,3},{5,4},{6,5},{7,6},{4,7},{9,8},{10,9},{11,1... | collective-permute-start | bytes 24584 | tf_op jit(solution)/shard_map/ppermute | solution.py:17
  161.8 36.2 %collective-permute-start.7 = (bf16[32,128]{1,0:T(8,128)(2,1)S(1)}, bf16[32,128]{1,0:T(8,128)(2,1)S(1)}, u32[]{:S(2)}, u32[]{:S(2)}) collective-permute-start(bf16[32,128]{1,0:T(8,128)(2,1)S(1)} %get-tuple-element.189), channel_id=1, source_target_pairs={{3,0},{0,1},{1,2},{2,3},{7,4},{4,5},{5,6},{6,7},{11,8},{8,9},{9,10... | collective-permute-start | bytes 24584 | tf_op jit(solution)/shard_map/ppermute | solution.py:17
  166.5 29.8 %copy-start.37 = (bf16[128]{0:T(256)(128)(2,1)S(1)}, bf16[128]{0:T(256)(128)(2,1)}, u32[]{:S(2)}) copy-start(bf16[128]{0:T(256)(128)(2,1)} %copy-done.36) | copy-start | bytes 772
  166.5 29.8 %copy-start.47 = (bf16[128,128]{1,0:T(8,128)(2,1)S(1)}, bf16[128,128]{1,0:T(8,128)(2,1)}, u32[]{:S(2)}) copy-start(bf16[128,128]{1,0:T(8,128)(2,1)} %param.33) | copy-start | bytes 98308
  166.5 32.9 %copy-start.19 = (bf16[128,128]{1,0:T(8,128)(2,1)S(1)}, bf16[128,128]{1,0:T(8,128)(2,1)}, u32[]{:S(2)}) copy-start(bf16[128,128]{1,0:T(8,128)(2,1)} %param.19) | copy-start | bytes 98308
  200.3 285.7 %copy-start.33 = (f32[1,2048]{1,0:T(1,128)S(1)}, f32[1,2048]{1,0:T(1,128)}, u32[]{:S(2)}) copy-start(f32[1,2048]{1,0:T(1,128)} %copy-done.32) | copy-start | bytes 24580
  200.3 285.7 %copy-start.35 = (f32[1,2048]{1,0:T(1,128)S(1)}, f32[1,2048]{1,0:T(1,128)}, u32[]{:S(2)}) copy-start(f32[1,2048]{1,0:T(1,128)} %copy-done.34) | copy-start | bytes 24580
  200.3 285.7 %copy-start.39 = (f32[128]{0:T(128)S(1)}, f32[128]{0:T(128)}, u32[]{:S(2)}) copy-start(f32[128]{0:T(128)} %copy-done.38) | copy-start | bytes 1540
  200.3 285.7 %copy-start.41 = (f32[128]{0:T(128)S(1)}, f32[128]{0:T(128)}, u32[]{:S(2)}) copy-start(f32[128]{0:T(128)} %copy-done.40) | copy-start | bytes 1540
  200.3 285.7 %copy-start.43 = (f32[128]{0:T(128)S(1)}, f32[128]{0:T(128)}, u32[]{:S(2)}) copy-start(f32[128]{0:T(128)} %copy-done.42) | copy-start | bytes 1540
  200.4 562.9 %all-reduce.5.cloned.1.call-start = ((), (), s32[]{:S(2)}) async-start(), calls=%async_computation | async-start | bytes 131072 | tf_op jit(solution)/shard_map/psum | solution.py:230
  (46 other events, 343.8 us)
Sparse Core Ops, SparseCore 0:
  200.5 285.4 all-reduce.6
  505.9 257.2 all-reduce.4
where the time goes:
time: 783 us; the launch traced here: 773 us
  waiting for transfers between devices  539 us (69%)
  matrix products  63.8 us (8%)
  local copies, waits for them, and re-layouts  59.7 us (8%)
  other arithmetic  58.6 us (7%)
  starting transfers between devices  36 us (5%)
  between operations  15.5 us (2%)
    psum x1, waiting for transfers between devices, long_range(): total_cos, total_sin = lax.psum((partial_cos, partial_sin), ('dx', 'dy'))  284 us
    psum x1, waiting for transfers between devices, local(): lax.psum((contract_rows(masked, grad_source), contract_rows(masked, grad_...  255 us
    gather x4, local copies, waits for them, and re-layouts, edge_geometry(): nearby = target_table[neighbour]  48.5 us
    scatter-add x2, other arithmetic, edge_backward(): table_part = jnp.zeros((target_table.shape[0], pair_grad.shape[2]), jnp.f...  45 us
    ppermute x8, starting transfers between devices, passed_along(): return lax.ppermute(block, axis, route)  35.8 us
    dot_general x11, matrix products, contract_rows(): lax.dot_general(left_side, right_side, (((0,), (0,)), ((), ())), preferre...  31.9 us
  transfers between devices with their start and end apart: 10, of which 2 were waited for; matrix products, arithmetic and copies ran while one was open for 8% of the time, Pallas kernels for 0%

commit v1 on v0

v1 whole, which is shorter than its diff:
```python
import math

import jax
import jax.numpy as jnp
from jax import lax
from jax.experimental import pallas as pl
from jax.experimental.pallas import tpu as pltpu
from jax.sharding import PartitionSpec as P

GEOMETRY = dict(y=8, z_hi=4, x=4, z_lo=2, core=2)
K = 2048
C = 128
A = 128
NB = 64
STEP = 8
COPIES = 100

BF = jnp.bfloat16
F32 = jnp.float32


def nn(a, b):
    return lax.dot_general(a, b, (((1,), (0,)), ((), ())), preferred_element_type=F32)


def nt(a, b):
    return lax.dot_general(a, b, (((1,), (1,)), ((), ())), preferred_element_type=F32)


def half_turns(f):
    q = f * f
    s = -0.007370430945714351
    for c in (
        0.08214588661112823,
        -0.5992645293207921,
        2.550164039877345,
        -5.16771278004997,
        3.141592653589793,
    ):
        s = s * q + c
    c0 = 0.0019295743094039231
    for c in (
        -0.02580689139001406,
        0.2353306303588935,
        -1.3352627688545893,
        4.058712126416768,
        -4.934802200544679,
        1.0,
    ):
        c0 = c0 * q + c
    return s * f, c0


def body(
    factor_scale,
    grad_scale,
    feat, pos, nbr, dist, ghost, counts, kvec, kw, sw, tw, ew, mw, cw, fw, cot,
    o_layer, o_feat, o_sg, o_tg, o_eg, o_mg, o_cg, o_fg,
    cs, part, full, rc, b1, rx, b2, ry, b3, rz,
    gout, gin, ggout, gret,
    g0, rgx, g1, rgy, g2, rgz, gfull,
    h0, rhy, h1, rhz, h2, rhx, hfull,
    nbr_t, gate_t, src_t, ga_t, tab_t, pick_t, agg_t, gs_t, tsum, epart,
    ssem, rsem,
):
    geo = GEOMETRY
    nx, ny, nc = geo["x"], geo["y"], geo["core"]
    nzl, nzh = geo["z_lo"], geo["z_hi"]
    nz = nzl * nzh
    ndx, ndy = ny * nzh * nx, nzl * nc
    dx, dy = lax.axis_index("dx"), lax.axis_index("dy")
    x = lax.rem(dx, nx)
    zh = lax.rem(lax.div(dx, nx), nzh)
    y = lax.div(dx, nx * nzh)
    zl, core = lax.div(dy, nc), lax.rem(dy, nc)
    z = zh * nzl + zl

    def device(px=None, py=None, pz=None, pc=None):
        px = x if px is None else px
        py = y if py is None else py
        pz = z if pz is None else pz
        pc = core if pc is None else pc
        return (
            (py * nzh + lax.div(pz, nzl)) * nx + px,
            lax.rem(pz, nzl) * nc + pc,
        )

    def ahead(me, d, n):
        return lax.rem(me + d, n)

    def x_peer(d):
        return device(px=ahead(x, d, nx))

    def y_peer(d):
        return device(py=ahead(y, d, ny))

    def z_peer(d):
        return device(pz=ahead(z, d, nz))

    def zc_peer(d):
        return device(pz=ahead(z, d // nc, nz), pc=ahead(core, d % nc, nc))

    def xc_peer(d):
        return device(px=ahead(x, d // nc, nx), pc=ahead(core, d % nc, nc))

    sibling = device(pc=ahead(core, 1, nc))
    faces = (
        (ahead(dx, 1, ndx), dy),
        (ahead(dx, ndx - 1, ndx), dy),
        (dx, ahead(dy, 1, ndy)),
        (dx, ahead(dy, ndy - 1, ndy)),
    )
    back = (faces[1], faces[0], faces[3], faces[2])

    barrier = pltpu.get_barrier_semaphore()
    greeted = list(faces)
    greeted += [y_peer(d) for d in range(1, ny)]
    greeted += [zc_peer(d) for d in range(1, nz * nc)]
    greeted += [xc_peer(d) for d in range(1, nx * nc) if d // nc]
    for other in greeted:
        pl.semaphore_signal(
            barrier, inc=1, device_id=other, device_id_type=pl.DeviceIdType.MESH
        )

    sent = []

    def send(src, dst, other):
        slot = len(sent)
        copy = pltpu.make_async_remote_copy(
            src_ref=src,
            dst_ref=dst,
            send_sem=ssem.at[slot],
            recv_sem=rsem.at[slot],
            device_id=other,
            device_id_type=pl.DeviceIdType.MESH,
        )
        copy.start()
        sent.append(copy)
        return copy

    def arrive(copies):
        for copy in copies:
            copy.wait_recv()

    def rows(ref, start, size):
        return ref.at[pl.ds(pl.multiple_of(start, 16), size)]

    def scatter(src, landing, me, n, size, peer):
        return [
            send(rows(src, ahead(me, d, n) * size, size), landing.at[d - 1], peer(d))
            for d in range(1, n)
        ]

    def collect(src, landing, me, n, size, dst):
        chunk = min(size, 128)

        def add(i, _):
            at = pl.multiple_of(i * chunk, 16)
            total = src[pl.ds(pl.multiple_of(me * size + at, 16), chunk), :].astype(F32)
            for d in range(1, n):
                total += landing[d - 1, pl.ds(at, chunk), :].astype(F32)
            dst[pl.ds(at, chunk), :] = total.astype(BF)
            return 0

        lax.fori_loop(0, size // chunk, add, 0)

    def share(landing, me, n, peer):
        return [send(landing.at[me], landing.at[me], peer(d)) for d in range(1, n)]

    def summed_slots(landing, n):
        total = landing[0].astype(F32)
        for d in range(1, n):
            total += landing[d].astype(F32)
        return total.astype(BF)

    def spread(ref, start, size, n, peer):
        return [
            send(rows(ref, start, size), rows(ref, start, size), peer(d)) for d in range(1, n)
        ]

    row_id = lax.broadcasted_iota(jnp.int32, (A, C), 0)
    alive = jnp.where(row_id < counts[0], 1.0, 0.0).astype(F32)
    masked32 = feat[...].astype(F32) * alive
    gm32 = cot[...].astype(F32) * alive
    masked, gm = masked32.astype(BF), gm32.astype(BF)
    masked_t = masked32.T.astype(BF)
    target = nn(masked, tw[...]).astype(BF)
    for f in range(4):
        pick_t[:, f * 32 : (f + 1) * 32] = jnp.where(
            lax.broadcasted_iota(jnp.int32, (A, 32), 0) == ghost[f : f + 1, :], 1.0, 0.0
        )
    pick = pick_t[...].T.astype(BF)
    gout[...] = nn(pick, target).astype(BF)

    pl.semaphore_wait(barrier, len(greeted))
    ghosts_in = [
        send(gout.at[pl.ds(f * 32, 32)], gin.at[pl.ds(f * 32, 32)], faces[f]) for f in range(4)
    ]

    cw_t = cw[...].astype(F32).T.astype(BF)
    values_t = jnp.concatenate([nt(cw_t, masked), nt(fw[...], gm)], axis=0).astype(BF)
    columns = [jnp.broadcast_to(pos[a : a + 1, :], (A, A)).T for a in range(3)]
    turn = 1.0 / (2.0 * math.pi)
    for block in range(K // 128):
        at = slice(block * 128, (block + 1) * 128)
        turns = (
            columns[0] * (kvec[0:1, at] * turn)
            + columns[1] * (kvec[1:2, at] * turn)
            + columns[2] * (kvec[2:3, at] * turn)
        )
        turns = turns - jnp.floor(turns + 0.5)
        s, c = half_turns(turns)
        cosine = (1.0 - 2.0 * s * s).astype(BF)
        sine = (2.0 * s * c).astype(BF)
        cs[:, at] = cosine
        cs[:, K + block * 128 : K + (block + 1) * 128] = sine
        part[block * 128 : (block + 1) * 128, :] = nn(values_t, cosine).astype(BF)
        part[K + block * 128 : K + (block + 1) * 128, :] = nn(values_t, sine).astype(BF)

    half = 2 * K // nc
    to_sibling = scatter(part, rc, core, nc, half, lambda d: sibling)

    src_t[...] = nn(masked, sw[...]).astype(BF).astype(F32).T
    ga_t[...] = nt(gm, mw[...]).astype(BF).astype(F32).T
    nbr_t[...] = nbr[...].astype(F32).T
    s, c = half_turns(dist[...] * 0.1)
    gate_t[...] = jnp.where(nbr[...] < 2 * A, c * c, 0.0).T
    tab_t[:, :A] = target.astype(F32).T.astype(BF)
    agg_t[...] = jnp.zeros_like(agg_t)
    gs_t[...] = jnp.zeros_like(gs_t)
    tsum[...] = jnp.zeros_like(tsum)
    epart[...] = jnp.zeros_like(epart)

    arrive(to_sibling)
    collect(part, rc, core, nc, half, b1)
    quarter = half // nx
    x_scatter = scatter(b1, rx, x, nx, quarter, x_peer)

    arrive(ghosts_in)
    tab_t[:, A:] = gin[...].astype(F32).T.astype(BF)

    ew_t = ew[...].astype(F32).T.astype(BF)

    def edge_step(step, _):
        table_row = lax.broadcasted_iota(jnp.int32, (2 * A, A), 0).astype(F32)
        hiddens, inners, picks, pairs = [], [], [], []
        agg_sum, gs_sum = agg_t[...], gs_t[...]
        source, upstream = src_t[...], ga_t[...]
        for pair in range(STEP // 2):
            base = step * STEP + 2 * pair
            gates = [gate_t[pl.ds(base + j, 1), :] for j in range(2)]
            chosen = jnp.concatenate(
                [
                    jnp.where(table_row == nbr_t[pl.ds(base + j, 1), :], 1.0, 0.0).astype(BF)
                    for j in range(2)
                ],
                axis=1,
            )
            summed = nn(tab_t[...], chosen) + jnp.concatenate([source, source], axis=1)
            g = 0.5 * jnp.tanh(0.5 * summed) + 0.5
            hidden = summed * g
            slope = g + hidden * (1.0 - g)
            hidden = hidden.astype(BF)
            mixed = nn(ew_t, hidden)
            g = 0.5 * jnp.tanh(0.5 * mixed) + 0.5
            message = mixed * g
            mixed_slope = g + message * (1.0 - g)
            agg_sum += gates[0] * message[:, :A] + gates[1] * message[:, A:]
            inner = jnp.concatenate(
                [
                    gates[0] * upstream * mixed_slope[:, :A],
                    gates[1] * upstream * mixed_slope[:, A:],
                ],
                axis=1,
            ).astype(BF)
            pair_grad = nn(ew[...], inner) * slope
            gs_sum += pair_grad[:, :A] + pair_grad[:, A:]
            hiddens.append(hidden)
            inners.append(inner)
            picks.append(chosen)
            pairs.append(pair_grad.astype(BF))
        agg_t[...] = agg_sum
        gs_t[...] = gs_sum
        epart[...] += nt(jnp.concatenate(hiddens, axis=1), jnp.concatenate(inners, axis=1))
        tsum[...] += nt(jnp.concatenate(picks, axis=1), jnp.concatenate(pairs, axis=1))
        return 0

    lax.fori_loop(0, NB // STEP, edge_step, 0)

    ggout[...] = tsum[A:, :].astype(BF)
    ghosts_back = [
        send(ggout.at[pl.ds(f * 32, 32)], gret.at[pl.ds(f * 32, 32)], back[f]) for f in range(4)
    ]

    arrive(x_scatter)
    collect(b1, rx, x, nx, quarter, b2)
    piece = quarter // ny
    y_scatter = scatter(b2, ry, y, ny, piece, y_peer)

    aggregate_t = agg_t[...].astype(BF)
    aggregate = agg_t[...].T.astype(BF)
    grad_source = gs_t[...].T.astype(BF)
    short_range = nn(aggregate, mw[...])
    g0[0:C, :] = nn(masked_t, grad_source).astype(BF)
    g0[2 * C : 3 * C, :] = epart[...].astype(BF)
    g0[3 * C :, :] = nn(aggregate_t, gm).astype(BF)
    arrive(ghosts_back)
    grad_target = (tsum[:A, :] + nn(pick_t[...].astype(BF), gret[...])).astype(BF)
    g0[C : 2 * C, :] = nn(masked_t, grad_target).astype(BF)
    gx, gy = 4 * C // nx, 4 * C // (nx * ny)
    g_x = scatter(g0, rgx, x, nx, gx, x_peer)
    short_grad = nt(grad_source, sw[...]) + nt(grad_target, tw[...])

    arrive(y_scatter)
    collect(b2, ry, y, ny, piece, b3)
    rz[pl.ds(z, 1)] = b3[...][None]
    z_share = share(rz, z, nz, z_peer)

    arrive(g_x)
    collect(g0, rgx, x, nx, gx, g1)
    g_y = scatter(g1, rgy, y, ny, gy, y_peer)

    arrive(z_share)
    mine = pl.multiple_of(core * half + x * quarter + y * piece, 16)
    full[pl.ds(mine, piece), :] = summed_slots(rz, nz)
    y_spread = spread(full, mine, piece, ny, y_peer)

    arrive(g_y)
    collect(g1, rgy, y, ny, gy, g2)
    zc = z * nc + core
    rgz[pl.ds(zc, 1)] = g2[...][None]
    g_zc = share(rgz, zc, nz * nc, zc_peer)

    arrive(y_spread)
    x_spread = spread(full, core * half + x * quarter, quarter, nx, x_peer)

    arrive(g_zc)
    g_mine = pl.multiple_of(x * gx + y * gy, 16)
    gfull[pl.ds(g_mine, gy), :] = summed_slots(rgz, nz * nc)
    g_ys = spread(gfull, g_mine, gy, ny, y_peer)

    arrive(x_spread)
    c_spread = spread(full, core * half, half, nc, lambda d: sibling)

    arrive(g_ys)
    g_xs = spread(gfull, x * gx, gx, nx, x_peer)

    arrive(c_spread)
    field = jnp.zeros((A, C), F32)
    for block in range(2 * K // 256):
        at = [slice(block * 256 + j * 128, block * 256 + (j + 1) * 128) for j in range(2)]
        factors = [
            kw[:, (a.start % K) : (a.start % K) + 128] * factor_scale for a in at
        ]
        weights = jnp.concatenate(
            [(full[a, :].astype(F32) * w).astype(BF) for a, w in zip(at, factors)], axis=1
        )
        field += nt(cs[:, block * 256 : (block + 1) * 256], weights)
    field = field.astype(BF).astype(F32)
    potential = field[:, :64].astype(BF)
    grad_charge = field[:, 64:].astype(BF)
    field_t = field.T.astype(BF)
    h0[:64, :] = nn(field_t[64:, :], masked).astype(BF)
    h0[64:, :] = nn(field_t[:64, :], gm).astype(BF)
    hy = C // ny
    h_y = scatter(h0, rhy, y, ny, hy, y_peer)

    o_layer[...] = (alive * (short_range + nn(potential, fw[...]))).astype(BF)
    o_feat[...] = (alive * (short_grad + nt(grad_charge, cw[...]))).astype(BF)
    arrive(g_xs)
    for i, out in enumerate((o_sg, o_tg, o_eg, o_mg)):
        out[...] = gfull[i * C : (i + 1) * C, :].astype(F32) * grad_scale

    arrive(h_y)
    collect(h0, rhy, y, ny, hy, h1)
    rhz[pl.ds(z, 1)] = h1[...][None]
    h_z = share(rhz, z, nz, z_peer)
    arrive(h_z)
    h2[...] = summed_slots(rhz, nz)
    xc = x * nc + core
    rhx[pl.ds(xc, 1)] = h2[...][None]
    h_x = share(rhx, xc, nx * nc, xc_peer)
    arrive(h_x)
    h_mine = pl.multiple_of(y * hy, 16)
    hfull[pl.ds(h_mine, hy), :] = summed_slots(rhx, nx * nc)
    arrive(spread(hfull, h_mine, hy, ny, y_peer))
    o_cg[...] = (hfull[:64, :].astype(F32) * grad_scale).T
    o_fg[...] = hfull[64:, :].astype(F32) * grad_scale

    for copy in sent:
        copy.wait_send()


def local(
    features, positions, neighbours, distances, ghost_rows, atom_counts, wavevectors,
    wave_weights, source_weight, target_weight, edge_weight, mix_weight, charge_weight,
    field_weight, cotangent,
):
    geo = GEOMETRY
    nx, ny, nc, nz = geo["x"], geo["y"], geo["core"], geo["z_lo"] * geo["z_hi"]
    total_atoms = A * lax.axis_size("dx") * lax.axis_size("dy")
    factor_scale = 4.0 / math.sqrt(total_atoms * K)
    grad_scale = 1.0 / math.sqrt(total_atoms)
    half = 2 * K // nc
    quarter = half // nx
    piece = quarter // ny
    gx, gy, hy = 4 * C // nx, 4 * C // (nx * ny), C // ny

    def bf(*shape):
        return pltpu.VMEM(shape, BF)

    def f32(*shape):
        return pltpu.VMEM(shape, F32)

    scratch = [
        bf(A, 2 * K), bf(2 * K, C), bf(2 * K, C),
        bf(nc - 1, half, C), bf(half, C),
        bf(nx - 1, quarter, C), bf(quarter, C),
        bf(ny - 1, piece, C), bf(piece, C),
        bf(nz, piece, C),
        bf(A, C), bf(A, C), bf(A, C), bf(A, C),
        bf(4 * C, C), bf(nx - 1, gx, C), bf(gx, C), bf(ny - 1, gy, C), bf(gy, C),
        bf(nz * nc, gy, C), bf(4 * C, C),
        bf(C, C), bf(ny - 1, hy, C), bf(hy, C), bf(nz, hy, C), bf(hy, C),
        bf(nx * nc, hy, C), bf(C, C),
        f32(NB, A), f32(NB, A), f32(C, A), f32(C, A), bf(C, 2 * A), f32(A, A),
        f32(C, A), f32(C, A), f32(2 * A, C), f32(C, C),
        pltpu.SemaphoreType.DMA((COPIES,)),
        pltpu.SemaphoreType.DMA((COPIES,)),
    ]
    vmem = pl.BlockSpec(memory_space=pltpu.VMEM)
    specs = [vmem] * 15
    specs[5] = pl.BlockSpec(memory_space=pltpu.SMEM)
    outs = [
        jax.ShapeDtypeStruct((A, C), BF),
        jax.ShapeDtypeStruct((A, C), BF),
        jax.ShapeDtypeStruct((C, C), F32),
        jax.ShapeDtypeStruct((C, C), F32),
        jax.ShapeDtypeStruct((C, C), F32),
        jax.ShapeDtypeStruct((C, C), F32),
        jax.ShapeDtypeStruct((C, 64), F32),
        jax.ShapeDtypeStruct((64, C), F32),
    ]

    def kernel(*refs):
        body(factor_scale, grad_scale, *refs)

    return pl.pallas_call(
        kernel,
        out_shape=outs,
        in_specs=specs,
        out_specs=[vmem] * 8,
        scratch_shapes=scratch,
        compiler_params=pltpu.CompilerParams(
            collective_id=0, has_side_effects=True, vmem_limit_bytes=40 * 1024 * 1024
        ),
        name="ewald_layer",
    )(
        features, positions, neighbours, distances, ghost_rows, atom_counts, wavevectors,
        wave_weights.reshape(1, K), source_weight, target_weight, edge_weight, mix_weight,
        charge_weight, field_weight, cotangent,
    )


def solution(mesh):
    atoms = P(("dx", "dy"), None)
    in_specs = (
        atoms, P(None, ("dx", "dy")), atoms, atoms, P(None, ("dx", "dy")), P(("dx", "dy")),
        P(), P(), P(), P(), P(), P(), P(), P(), atoms,
    )
    out_specs = (atoms, atoms, P(), P(), P(), P(), P(), P())
    return jax.shard_map(
        local, mesh=mesh, in_specs=in_specs, out_specs=out_specs, check_vma=False
    )
```

time: 783 us -> 89.1 us (0.11); the launches traced: 773 us -> 88.7 us
  waiting for transfers between devices: 539 us -> 0 us
  Pallas kernels: 0 us -> 78.2 us
  matrix products: 63.8 us -> 0 us
  other arithmetic: 58.6 us -> 0 us
  local copies, waits for them, and re-layouts: 59.7 us -> 9.05 us
  starting transfers between devices: 36 us -> 0 us
  between operations: 15.5 us -> 1.47 us
    psum x2 -> x0, waiting for transfers between devices: 539 us -> none  [the longest x1 284 us: long_range(): total_cos, total_sin = lax.psum((partial_cos, partial_sin), ('dx', 'dy'))]
    pallas_call x0 -> x1, Pallas kernels: none -> 78.2 us  [local(): pl.pallas_call(kernel, out_shape=outs, in_specs=specs, out_specs=[vmem] *...]
    dot_general x31 -> x0, matrix products: 63.8 us -> none  [the longest x11 31.9 us: contract_rows(): lax.dot_general(left_side, right_side, (((0,), (0,)), ((), ())), preferre...]
    gather x5 -> x0, local copies, waits for them, and re-layouts: 49.2 us -> none  [the longest x4 48.5 us: edge_geometry(): nearby = target_table[neighbour]]
    scatter-add x3 -> x0, other arithmetic: 46.4 us -> none  [the longest x2 45 us: edge_backward(): table_part = jnp.zeros((target_table.shape[0], pair_grad.shape[2]), jnp.f...]
    ppermute x8 -> x0, starting transfers between devices: 35.8 us -> none  [passed_along(): return lax.ppermute(block, axis, route)]
  transfers between devices with their start and end apart: 10 -> 0, of which waited for: 2 -> 0; matrix products, arithmetic and copies ran while one was open for 8% -> 0% of each run, Pallas kernels for 0% -> 0%
where the time goes in v1:
time: 89.1 us; the launch traced here: 88.7 us
  Pallas kernels  78.2 us (88%)
  local copies, waits for them, and re-layouts  9.05 us (10%)
  between operations  1.47 us (2%)
    pallas_call x1, Pallas kernels, local(): pl.pallas_call(kernel, out_shape=outs, in_specs=specs, out_specs=[vmem] *...  78.2 us
    unnamed x32, local copies, waits for them, and re-layouts  8.35 us

profile of v1, /device:TPU:1, one launch (start us, length us, event | category | flops | bytes accessed | tf_op | source)
XLA Modules:
  0.0 88.7 jit_solution(1669881594796322064)
XLA Ops:
  1.3 0.8 copy.25.refs_12_
  2.2 0.0 copy-start.3
  2.2 0.0 copy-start.4
  2.2 0.0 copy-start.5
  2.2 0.9 copy.23.refs_2_
  3.1 0.0 copy-start
  3.1 0.0 copy-start.1
  3.1 0.0 copy-start.2
  3.1 0.9 copy.24.refs_3_
  4.0 0.0 copy-done.9
  4.0 0.0 copy-done.6
  4.0 0.0 copy-done.7
  4.1 0.0 copy-start.8
  4.1 0.7 copy-done.8
  4.8 0.7 copy-done.10
  5.4 78.2 %ewald_layer.1 = (bf16[128,128]{1,0:T(8,128)(2,1)S(1)}, bf16[128,128]{1,0:T(8,128)(2,1)S(1)}, f32[128,128]{1,0:T(8,128)S(1)}, f32[128,128]{1,0:T(8,128)S(1)}, f3...) custom-call(bf16[128,128]{1,0:T(8,128)(2,1)S(1)} %copy-done, ...), custom_call_target="tpu_custom_call" | custom-call | tf_op jit(solution)/shard_map/ewald_layer/pallas_call | solution.py:448
  83.6 0.7 copy.26
  84.3 0.6 copy.35
  84.9 0.6 copy.36
  85.5 0.6 copy.37
  86.2 0.6 copy.38
  86.8 0.6 copy.39
  87.4 0.6 copy.40
  88.1 0.6 copy.41
  (10 shorter events, 0.0 us)
Async XLA Ops:
  0.6 3.3 %copy-start.9 = (f32[3,128]{1,0:T(4,128)S(1)}, f32[3,128]{1,0:T(4,128)}, u32[]{:S(2)}) copy-start(f32[3,128]{1,0:T(4,128)} %refs_1_.1) | copy-start | bytes 4612
  1.3 2.7 %copy-start.6 = (bf16[128,128]{1,0:T(8,128)(2,1)S(1)}, bf16[128,128]{1,0:T(8,128)(2,1)}, u32[]{:S(2)}) copy-start(bf16[128,128]{1,0:T(8,128)(2,1)} %refs_14_.1) | copy-start | bytes 98308
  1.3 2.7 %copy-start.7 = (bf16[64,128]{1,0:T(8,128)(2,1)S(1)}, bf16[64,128]{1,0:T(8,128)(2,1)}, u32[]{:S(2)}) copy-start(bf16[64,128]{1,0:T(8,128)(2,1)} %refs_13_.1) | copy-start | bytes 49156
  2.2 1.8 %copy-start.3 = (bf16[128,128]{1,0:T(8,128)(2,1)S(1)}, bf16[128,128]{1,0:T(8,128)(2,1)}, u32[]{:S(2)}) copy-start(bf16[128,128]{1,0:T(8,128)(2,1)} %refs_9_.1) | copy-start | bytes 98308
  2.2 1.8 %copy-start.4 = (bf16[128,128]{1,0:T(8,128)(2,1)S(1)}, bf16[128,128]{1,0:T(8,128)(2,1)}, u32[]{:S(2)}) copy-start(bf16[128,128]{1,0:T(8,128)(2,1)} %refs_10_.1) | copy-start | bytes 98308
  2.2 1.8 %copy-start.5 = (bf16[128,128]{1,0:T(8,128)(2,1)S(1)}, bf16[128,128]{1,0:T(8,128)(2,1)}, u32[]{:S(2)}) copy-start(bf16[128,128]{1,0:T(8,128)(2,1)} %refs_11_.1) | copy-start | bytes 98308
  3.1 1.0 %copy-start = (bf16[128,128]{1,0:T(8,128)(2,1)S(1)}, bf16[128,128]{1,0:T(8,128)(2,1)}, u32[]{:S(2)}) copy-start(bf16[128,128]{1,0:T(8,128)(2,1)} %refs_0_.1) | copy-start | bytes 98308
  3.1 1.0 %copy-start.1 = (f32[3,2048]{1,0:T(4,128)S(1)}, f32[3,2048]{1,0:T(4,128)}, u32[]{:S(2)}) copy-start(f32[3,2048]{1,0:T(4,128)} %refs_6_.1) | copy-start | bytes 73732
  3.1 1.0 %copy-start.2 = (bf16[128,128]{1,0:T(8,128)(2,1)S(1)}, bf16[128,128]{1,0:T(8,128)(2,1)}, u32[]{:S(2)}) copy-start(bf16[128,128]{1,0:T(8,128)(2,1)} %refs_8_.1) | copy-start | bytes 98308
  4.1 0.7 copy-start.8
  4.8 0.7 copy-start.10

commit v2 on v1

v2 whole, which is shorter than its diff:
```python
import math

import jax
import jax.numpy as jnp
from jax import lax
from jax.experimental import pallas as pl
from jax.experimental.pallas import tpu as pltpu
from jax.sharding import PartitionSpec as P

GEOMETRY = dict(y=8, z_hi=4, x=4, z_lo=2, core=2)
K = 2048
C = 128
A = 128
NB = 64
STEP = 8
COPIES = 140
ROWS = (1024, 512, 512)

FIRST = (0, 14, 4, 5, 1)
LATER = (6, 7, 2, 3, 8, 9, 10, 11, 12, 13)

BF = jnp.bfloat16
F32 = jnp.float32


def nn(a, b):
    return lax.dot_general(a, b, (((1,), (0,)), ((), ())), preferred_element_type=F32)


def nt(a, b):
    return lax.dot_general(a, b, (((1,), (1,)), ((), ())), preferred_element_type=F32)


def half_turns(f):
    q = f * f
    s = -0.007370430945714351
    for c in (
        0.08214588661112823,
        -0.5992645293207921,
        2.550164039877345,
        -5.16771278004997,
        3.141592653589793,
    ):
        s = s * q + c
    c0 = 0.0019295743094039231
    for c in (
        -0.02580689139001406,
        0.2353306303588935,
        -1.3352627688545893,
        4.058712126416768,
        -4.934802200544679,
        1.0,
    ):
        c0 = c0 * q + c
    return s * f, c0


def body(
    factor_scale,
    grad_scale,
    operands,
    out,
    held, held_sem,
    x_out, x_in, pos_out, pos_in, kv, sums,
    la, ta, lb, tb, lc, tc, la2, lb2, lc2, t2, lz, ly, fin,
    w_out, w_in, w_full, cosine, sine, e_out, e_in,
    gout, gin, ggout, gret,
    g0, rgx, g1, rgy, g2, rgz, gfull,
    rhy, rhz, rhx, h2, h_in,
    nbr_t, gate_t, src_t, ga_t, tab_t, pick_t, agg_t, gs_t, tsum, epart,
    ssem, rsem,
):
    fetch = [
        pltpu.make_async_copy(src, dst, held_sem.at[i])
        for i, (src, dst) in enumerate(zip(operands, held))
    ]
    for i in FIRST + LATER:
        fetch[i].start()
    feat, pos, nbr, dist, ghost, counts, kvec, kw, sw, tw, ew, mw, cw, fw, cot = held

    geo = GEOMETRY
    nx, ny, nc = geo["x"], geo["y"], geo["core"]
    nzl, nzh = geo["z_lo"], geo["z_hi"]
    nz = nzl * nzh
    ndx, ndy = ny * nzh * nx, nzl * nc
    dx, dy = lax.axis_index("dx"), lax.axis_index("dy")
    x = lax.rem(dx, nx)
    zh = lax.rem(lax.div(dx, nx), nzh)
    y = lax.div(dx, nx * nzh)
    zl, core = lax.div(dy, nc), lax.rem(dy, nc)
    z = zh * nzl + zl

    def device(px=None, py=None, pz=None, pc=None):
        px = x if px is None else px
        py = y if py is None else py
        pz = z if pz is None else pz
        pc = core if pc is None else pc
        return (
            (py * nzh + lax.div(pz, nzl)) * nx + px,
            lax.rem(pz, nzl) * nc + pc,
        )

    def ahead(me, d, n):
        return lax.rem(me + d, n)

    def x_peer(d):
        return device(px=ahead(x, d, nx))

    def y_peer(d):
        return device(py=ahead(y, d, ny))

    def z_peer(d):
        return device(pz=ahead(z, d, nz))

    def zc_peer(d):
        return device(pz=ahead(z, d // nc, nz), pc=ahead(core, d % nc, nc))

    sibling = device(pc=ahead(core, 1, nc))
    faces = (
        (ahead(dx, 1, ndx), dy),
        (ahead(dx, ndx - 1, ndx), dy),
        (dx, ahead(dy, 1, ndy)),
        (dx, ahead(dy, ndy - 1, ndy)),
    )
    back = (faces[1], faces[0], faces[3], faces[2])

    barrier = pltpu.get_barrier_semaphore()
    greeted = list(faces)
    greeted += [x_peer(d) for d in range(1, nx)]
    greeted += [y_peer(d) for d in range(1, ny)]
    greeted += [zc_peer(d) for d in range(1, nz * nc)]
    for other in greeted:
        pl.semaphore_signal(
            barrier, inc=1, device_id=other, device_id_type=pl.DeviceIdType.MESH
        )

    sent = []

    def send(src, dst, other):
        slot = len(sent)
        copy = pltpu.make_async_remote_copy(
            src_ref=src,
            dst_ref=dst,
            send_sem=ssem.at[slot],
            recv_sem=rsem.at[slot],
            device_id=other,
            device_id_type=pl.DeviceIdType.MESH,
        )
        copy.start()
        sent.append(copy)
        return copy

    def arrive(copies):
        for copy in copies:
            copy.wait_recv()

    def rows(ref, start, size):
        return ref.at[pl.ds(pl.multiple_of(start, 16), size)]

    def scatter(src, base, landing, me, n, size, peer):
        return [
            send(rows(src, base + ahead(me, d, n) * size, size), landing.at[d - 1], peer(d))
            for d in range(1, n)
        ]

    def collect(src, base, landing, me, n, size, dst, dst_base=0):
        chunk = min(size, 128)

        def add(i, _):
            at = pl.multiple_of(i * chunk, 16)
            total = src[pl.ds(pl.multiple_of(base + me * size + at, 16), chunk), :].astype(F32)
            for d in range(1, n):
                total += landing[d - 1, pl.ds(at, chunk), :].astype(F32)
            dst[pl.ds(pl.multiple_of(dst_base + at, 16), chunk), :] = total.astype(BF)
            return 0

        if size == chunk:
            add(0, 0)
        else:
            lax.fori_loop(0, size // chunk, add, 0)

    def share(landing, me, n, peer):
        return [send(landing.at[me], landing.at[me], peer(d)) for d in range(1, n)]

    def summed_slots(landing, n):
        total = landing[0].astype(F32)
        for d in range(1, n):
            total += landing[d].astype(F32)
        return total

    def spread(ref, start, size, n, peer):
        return [
            send(rows(ref, start, size), rows(ref, start, size), peer(d)) for d in range(1, n)
        ]

    first_core = jnp.where(core == 0, 1.0, 0.0).astype(F32)

    def by_core(mine_if_first, mine_if_second):
        return first_core * mine_if_first + (1.0 - first_core) * mine_if_second

    for i in FIRST:
        fetch[i].wait()

    row_id = lax.broadcasted_iota(jnp.int32, (A, C), 0)
    alive = jnp.where(row_id < counts[0], 1.0, 0.0).astype(F32)
    masked32 = feat[...].astype(F32) * alive
    gm32 = cot[...].astype(F32) * alive
    masked, gm = masked32.astype(BF), gm32.astype(BF)
    for f in range(4):
        pick_t[:, f * 32 : (f + 1) * 32] = jnp.where(
            lax.broadcasted_iota(jnp.int32, (A, 32), 0) == ghost[f : f + 1, :], 1.0, 0.0
        )
    gout[...] = nn(pick_t[...].T.astype(BF), masked).astype(BF)
    x_out[...] = by_core(gm32, masked32).astype(BF)
    pos_out[...] = jnp.zeros_like(pos_out)
    pos_out[0:3, :] = pos[...]

    pl.semaphore_wait(barrier, len(greeted))
    atoms_in = [send(x_out, x_in, sibling), send(pos_out, pos_in, sibling)]
    ghosts_in = [
        send(gout.at[pl.ds(f * 32, 32)], gin.at[pl.ds(f * 32, 32)], faces[f]) for f in range(4)
    ]

    for i in LATER:
        fetch[i].wait()

    masked_t = masked32.T.astype(BF)
    kv[...] = jnp.zeros_like(kv)
    kv[0:3, :] = kvec[...] * (1.0 / (2.0 * math.pi))
    kv[3:4, :] = jnp.sqrt(kw[...] * factor_scale)
    own_kind = by_core(masked32, gm32).astype(BF)

    src_t[...] = nn(masked, sw[...]).astype(BF).astype(F32).T
    ga_t[...] = nt(gm, mw[...]).astype(BF).astype(F32).T
    nbr_t[...] = nbr[...].astype(F32)
    s, c = half_turns(dist[...] * 0.1)
    gate_t[...] = jnp.where(nbr[...] < 2 * A, c * c, 0.0)
    tab_t[:, :A] = nn(masked, tw[...]).astype(BF).astype(F32).T.astype(BF)
    agg_t[...] = jnp.zeros_like(agg_t)
    gs_t[...] = jnp.zeros_like(gs_t)
    tsum[...] = jnp.zeros_like(tsum)
    epart[...] = jnp.zeros_like(epart)
    ew_t = ew[...].astype(F32).T.astype(BF)

    arrive(atoms_in)
    both = jnp.concatenate([own_kind, x_in[...]], axis=0)
    spots = [
        jnp.concatenate([pos[a : a + 1, :], pos_in[a : a + 1, :]], axis=1) for a in range(3)
    ]

    def waves(turns, root):
        turns = turns - jnp.floor(turns + 0.5)
        s, c = half_turns(turns)
        return ((1.0 - 2.0 * s * s) * root).astype(BF), ((2.0 * s * c) * root).astype(BF)

    def sum_block(block, _):
        at = pl.multiple_of(block * 128, 128)
        cols = kv[:, pl.ds(at, 128)].T
        turns = cols[:, 0:1] * spots[0] + cols[:, 1:2] * spots[1] + cols[:, 2:3] * spots[2]
        cos_t, sin_t = waves(turns, cols[:, 3:4])
        sums[pl.ds(at, 128), :C] = nn(cos_t, both).astype(BF)
        sums[pl.ds(at, 128), C:] = nn(sin_t, both).astype(BF)
        return 0

    base_a, base_b, base_c = 0, ROWS[0], ROWS[0] + ROWS[1]
    a1, b1, c1 = ROWS[0] // nx, ROWS[1] // ny, ROWS[2] // nz
    a2, b2, c2 = a1 // ny, b1 // nx, c1 // nx
    lax.fori_loop(0, base_b // 128, sum_block, 0)
    first_a = scatter(sums, base_a, la, x, nx, a1, x_peer)
    lax.fori_loop(base_b // 128, base_c // 128, sum_block, 0)
    first_b = scatter(sums, base_b, lb, y, ny, b1, y_peer)
    lax.fori_loop(base_c // 128, K // 128, sum_block, 0)
    first_c = scatter(sums, base_c, lc, z, nz, c1, z_peer)

    arrive(ghosts_in)
    ghosts = gin[...]
    tab_t[:, A:] = nn(ghosts, tw[...]).astype(BF).astype(F32).T.astype(BF)
    table_t = jnp.concatenate([masked_t, ghosts.astype(F32).T.astype(BF)], axis=1)
    def edge_step(step, _):
        table_row = lax.broadcasted_iota(jnp.int32, (2 * A, A), 0).astype(F32)
        hiddens, inners, picks, pairs = [], [], [], []
        agg_sum, gs_sum = agg_t[...], gs_t[...]
        source, upstream = src_t[...], ga_t[...]
        for pair in range(STEP // 2):
            base = step * STEP + 2 * pair
            gates = [gate_t[pl.ds(base + j, 1), :] for j in range(2)]
            chosen = jnp.concatenate(
                [
                    jnp.where(table_row == nbr_t[pl.ds(base + j, 1), :], 1.0, 0.0).astype(BF)
                    for j in range(2)
                ],
                axis=1,
            )
            summed = nn(tab_t[...], chosen) + jnp.concatenate([source, source], axis=1)
            g = 0.5 * jnp.tanh(0.5 * summed) + 0.5
            hidden = summed * g
            slope = g + hidden * (1.0 - g)
            hidden = hidden.astype(BF)
            mixed = nn(ew_t, hidden)
            g = 0.5 * jnp.tanh(0.5 * mixed) + 0.5
            message = mixed * g
            mixed_slope = g + message * (1.0 - g)
            agg_sum += gates[0] * message[:, :A] + gates[1] * message[:, A:]
            inner = jnp.concatenate(
                [
                    gates[0] * upstream * mixed_slope[:, :A],
                    gates[1] * upstream * mixed_slope[:, A:],
                ],
                axis=1,
            ).astype(BF)
            pair_grad = nn(ew[...], inner) * slope
            gs_sum += pair_grad[:, :A] + pair_grad[:, A:]
            hiddens.append(hidden)
            inners.append(inner)
            picks.append(chosen)
            pairs.append(pair_grad.astype(BF))
        agg_t[...] = agg_sum
        gs_t[...] = gs_sum
        epart[...] += nt(jnp.concatenate(hiddens, axis=1), jnp.concatenate(inners, axis=1))
        tsum[...] += nt(jnp.concatenate(picks, axis=1), jnp.concatenate(pairs, axis=1))
        return 0

    steps = NB // STEP
    cut = (steps // 2, steps - 1)
    lax.fori_loop(0, cut[0], edge_step, 0)
    arrive(first_a)
    collect(sums, base_a, la, x, nx, a1, ta)
    second_a = scatter(ta, 0, la2, y, ny, a2, y_peer)
    arrive(first_b)
    collect(sums, base_b, lb, y, ny, b1, tb)
    second_b = scatter(tb, 0, lb2, x, nx, b2, x_peer)
    arrive(first_c)
    collect(sums, base_c, lc, z, nz, c1, tc)
    second_c = scatter(tc, 0, lc2, x, nx, c2, x_peer)

    lax.fori_loop(cut[0], cut[1], edge_step, 0)
    ab2 = a2 + b2
    arrive(second_b)
    collect(tb, 0, lb2, x, nx, b2, t2, a2)
    arrive(second_c)
    collect(tc, 0, lc2, x, nx, c2, t2, ab2)
    ly[pl.ds(y, 1)] = t2[ab2:, :][None]
    third_c = share(ly, y, ny, y_peer)
    arrive(second_a)
    collect(ta, 0, la2, y, ny, a2, t2, 0)
    lz[pl.ds(z, 1)] = t2[:ab2, :][None]
    third_ab = share(lz, z, nz, z_peer)

    lax.fori_loop(cut[1], steps, edge_step, 0)

    table_sum = tsum[...]
    ggout[...] = table_sum[A:, :].astype(BF)
    ghosts_back = [
        send(ggout.at[pl.ds(f * 32, 32)], gret.at[pl.ds(f * 32, 32)], back[f]) for f in range(4)
    ]
    aggregate_t = agg_t[...].astype(BF)
    grad_source = gs_t[...].T.astype(BF)
    g0[0:C, :] = nn(masked_t, grad_source).astype(BF)
    g0[C : 2 * C, :] = nn(table_t, table_sum.astype(BF)).astype(BF)
    g0[2 * C : 3 * C, :] = epart[...].astype(BF)
    g0[3 * C :, :] = nn(aggregate_t, gm).astype(BF)
    gx, gy = 4 * C // nx, 4 * C // (nx * ny)
    g_x = scatter(g0, 0, rgx, x, nx, gx, x_peer)

    fw_t = fw[...].astype(F32).T
    project = by_core(cw[...].astype(F32).T, fw_t).astype(BF)
    none = jnp.zeros((C, 64), BF)
    project = jnp.concatenate(
        [
            jnp.concatenate([project, none], axis=1),
            jnp.concatenate([none, project], axis=1),
        ],
        axis=0,
    )
    arrive(third_c)
    fin[ab2:, :] = summed_slots(ly, ny).astype(BF)
    arrive(third_ab)
    fin[:ab2, :] = summed_slots(lz, nz).astype(BF)
    w_out[...] = nn(fin[...], project).astype(BF)
    place_a = pl.multiple_of(base_a + x * a1 + y * a2, 16)
    place_b = pl.multiple_of(base_b + y * b1 + x * b2, 16)
    place_c = pl.multiple_of(base_c + z * c1 + x * c2, 16)
    w_full[pl.ds(place_a, a2), :] = w_out[:a2, :]
    w_full[pl.ds(place_b, b2), :] = w_out[a2:ab2, :]
    w_full[pl.ds(place_c, c2), :] = w_out[ab2:, :]
    spread_a = spread(w_full, place_a, a2, ny, y_peer)
    spread_b = spread(w_full, place_b, b2, nx, x_peer)
    spread_c = spread(w_full, place_c, c2, nx, x_peer)
    w_swap = [send(w_out, w_in, sibling)]

    arrive(g_x)
    collect(g0, 0, rgx, x, nx, gx, g1)
    g_y = scatter(g1, 0, rgy, y, ny, gy, y_peer)

    arrive(w_swap)
    other_t = w_in[...].astype(F32).T
    in_ab = lax.broadcasted_iota(jnp.int32, other_t.shape, 1) < ab2

    def weight_part(left):
        quads = nn(left.astype(BF), fin[...])
        return (quads[:64, :C] + quads[64:, C:]).astype(BF)

    rhy[pl.ds(y, 1)] = weight_part(jnp.where(in_ab, other_t, 0.0))[None]
    rhz[pl.ds(z, 1)] = weight_part(jnp.where(in_ab, 0.0, other_t))[None]

    arrive(spread_b)
    spread_b = spread(w_full, base_b + y * b1, b1, ny, y_peer)
    arrive(spread_c)
    spread_c = spread(w_full, base_c + z * c1, c1, nz, z_peer)
    h_y = share(rhy, y, ny, y_peer)
    h_z = share(rhz, z, nz, z_peer)
    arrive(spread_a)
    spread_a = spread(w_full, base_a + x * a1, a1, nx, x_peer)

    spot_cols = [
        jnp.concatenate(
            [
                jnp.broadcast_to(pos[a : a + 1, :], (A, A)).T,
                jnp.broadcast_to(pos_in[a : a + 1, :], (A, A)).T,
            ],
            axis=0,
        )
        for a in range(3)
    ]

    def wave_block(block, _):
        at = pl.ds(pl.multiple_of(block * 128, 128), 128)
        turns = (
            spot_cols[0] * kv[0:1, at] + spot_cols[1] * kv[1:2, at] + spot_cols[2] * kv[2:3, at]
        )
        cosine[:, at], sine[:, at] = waves(turns, kv[3:4, at])
        return 0

    lax.fori_loop(0, K // 128, wave_block, 0)

    arrive(g_y)
    collect(g1, 0, rgy, y, ny, gy, g2)
    zc = z * nc + core
    rgz[pl.ds(zc, 1)] = g2[...][None]
    g_zc = share(rgz, zc, nz * nc, zc_peer)

    arrive(ghosts_back)
    grad_target = (table_sum[:A, :] + nn(pick_t[...].astype(BF), gret[...])).astype(BF)
    short_grad = nt(grad_source, sw[...]) + nt(grad_target, tw[...])
    short_range = nn(agg_t[...].T.astype(BF), mw[...])

    arrive(h_y)
    arrive(h_z)
    rhx[pl.ds(x, 1)] = (summed_slots(rhy, ny) + summed_slots(rhz, nz)).astype(BF)[None]
    h_x = share(rhx, x, nx, x_peer)

    arrive(spread_b)
    arrive(spread_c)
    arrive(spread_a)
    field = nn(cosine[...], w_full[...]) + pltpu.roll(nn(sine[...], w_full[...]), 64, 1)
    e_out[...] = field[A:, :].astype(BF)
    e_swap = [send(e_out, e_in, sibling)]

    arrive(g_zc)
    g_mine = pl.multiple_of(x * gx + y * gy, 16)
    gfull[pl.ds(g_mine, gy), :] = summed_slots(rgz, nz * nc).astype(BF)
    g_ys = spread(gfull, g_mine, gy, ny, y_peer)

    arrive(h_x)
    h2[...] = summed_slots(rhx, nx).astype(BF)
    h_swap = [send(h2, h_in, sibling)]

    arrive(e_swap)
    here = field[:A, :].astype(BF).astype(F32)
    there = e_in[...].astype(F32)
    potential = by_core(here, there).astype(BF)[:, :64]
    grad_charge = by_core(there, here).astype(BF)[:, :64]
    out[0:A, :] = alive * (short_range + nn(potential, fw[...]))
    out[A : 2 * A, :] = alive * (short_grad + nn(grad_charge, cw[...]))

    arrive(h_swap)
    here, there = h2[...].astype(F32), h_in[...].astype(F32)
    out[6 * C : 6 * C + 64, :] = by_core(here, there) * grad_scale
    out[6 * C + 64 : 7 * C, :] = by_core(there, here) * grad_scale

    arrive(g_ys)
    g_xs = spread(gfull, x * gx, gx, nx, x_peer)
    arrive(g_xs)
    out[2 * C : 6 * C, :] = gfull[...].astype(F32) * grad_scale

    for copy in sent:
        copy.wait_send()


def place(
    rows, o_layer, o_feat, o_sg, o_tg, o_eg, o_mg, o_cg, o_fg, layer, feat, sem
):
    layer[...] = rows[0:A, :].astype(BF)
    feat[...] = rows[A : 2 * A, :].astype(BF)
    moves = [(layer, o_layer), (feat, o_feat)]
    moves += [
        (rows.at[pl.ds((i + 2) * C, C)], out) for i, out in enumerate((o_sg, o_tg, o_eg, o_mg))
    ]
    moves += [(rows.at[pl.ds(6 * C, 64)], o_cg), (rows.at[pl.ds(6 * C + 64, 64)], o_fg)]
    copies = [pltpu.make_async_copy(a, b, sem.at[i]) for i, (a, b) in enumerate(moves)]
    for copy in copies:
        copy.start()
    for copy in copies:
        copy.wait()


def local(
    features, positions, neighbours, distances, ghost_rows, atom_counts, wavevectors,
    wave_weights, source_weight, target_weight, edge_weight, mix_weight, charge_weight,
    field_weight, cotangent,
):
    geo = GEOMETRY
    nx, ny, nc, nz = geo["x"], geo["y"], geo["core"], geo["z_lo"] * geo["z_hi"]
    total_atoms = A * lax.axis_size("dx") * lax.axis_size("dy")
    factor_scale = 4.0 / math.sqrt(total_atoms * K)
    grad_scale = 1.0 / math.sqrt(total_atoms)
    a1, b1, c1 = ROWS[0] // nx, ROWS[1] // ny, ROWS[2] // nz
    a2, b2, c2 = a1 // ny, b1 // nx, c1 // nx
    last = a2 + b2 + c2
    gx, gy = 4 * C // nx, 4 * C // (nx * ny)

    def bf(*shape):
        return pltpu.VMEM(shape, BF)

    def f32(*shape):
        return pltpu.VMEM(shape, F32)

    scratch = [
        bf(A, C), bf(A, C), f32(8, A), f32(8, A), f32(8, K), bf(K, 2 * C),
        bf(nx - 1, a1, 2 * C), bf(a1, 2 * C),
        bf(ny - 1, b1, 2 * C), bf(b1, 2 * C),
        bf(nz - 1, c1, 2 * C), bf(c1, 2 * C),
        bf(ny - 1, a2, 2 * C), bf(nx - 1, b2, 2 * C), bf(nx - 1, c2, 2 * C),
        bf(last, 2 * C), bf(nz, a2 + b2, 2 * C), bf(ny, c2, 2 * C), bf(last, 2 * C),
        bf(last, C), bf(last, C), bf(K, C), bf(2 * A, K), bf(2 * A, K), bf(A, C), bf(A, C),
        bf(A, C), bf(A, C), bf(A, C), bf(A, C),
        bf(4 * C, C), bf(nx - 1, gx, C), bf(gx, C), bf(ny - 1, gy, C), bf(gy, C),
        bf(nz * nc, gy, C), bf(4 * C, C),
        bf(ny, 64, C), bf(nz, 64, C), bf(nx, 64, C), bf(64, C), bf(64, C),
        f32(NB, A), f32(NB, A), f32(C, A), f32(C, A), bf(C, 2 * A), f32(A, A),
        f32(C, A), f32(C, A), f32(2 * A, C), f32(C, C),
        pltpu.SemaphoreType.DMA((COPIES,)),
        pltpu.SemaphoreType.DMA((COPIES,)),
    ]
    vmem = pl.BlockSpec(memory_space=pltpu.VMEM)
    anywhere = pl.BlockSpec(memory_space=pl.ANY)
    operands = (
        features, positions, neighbours.T, distances.T, ghost_rows, atom_counts, wavevectors,
        wave_weights.reshape(1, K), source_weight, target_weight, edge_weight, mix_weight,
        charge_weight.T, field_weight, cotangent,
    )
    n_in = len(operands)
    held = [
        pltpu.SMEM(a.shape, a.dtype) if a.ndim == 1 else pltpu.VMEM(a.shape, a.dtype)
        for a in operands
    ]

    def kernel(*refs):
        left = refs[n_in + 1 :]
        body(factor_scale, grad_scale, refs[:n_in], refs[n_in], left[:n_in], *left[n_in:])

    rows = pl.pallas_call(
        kernel,
        out_shape=jax.ShapeDtypeStruct((7 * C, C), F32),
        in_specs=[anywhere] * n_in,
        out_specs=vmem,
        scratch_shapes=held + [pltpu.SemaphoreType.DMA((n_in,))] + scratch,
        compiler_params=pltpu.CompilerParams(
            collective_id=0, has_side_effects=True, vmem_limit_bytes=60 * 1024 * 1024
        ),
        name="ewald_layer",
    )(*operands)
    outs = pl.pallas_call(
        place,
        out_shape=[jax.ShapeDtypeStruct((A, C), BF)] * 2
        + [jax.ShapeDtypeStruct((C, C), F32)] * 4
        + [jax.ShapeDtypeStruct((64, C), F32)] * 2,
        in_specs=[vmem],
        out_specs=[anywhere] * 8,
        scratch_shapes=[bf(A, C), bf(A, C), pltpu.SemaphoreType.DMA((8,))],
        name="place_outputs",
    )(rows)
    return (*outs[:6], outs[6].T, outs[7])


def solution(mesh):
    atoms = P(("dx", "dy"), None)
    in_specs = (
        atoms, P(None, ("dx", "dy")), atoms, atoms, P(None, ("dx", "dy")), P(("dx", "dy")),
        P(), P(), P(), P(), P(), P(), P(), P(), atoms,
    )
    out_specs = (atoms, atoms, P(), P(), P(), P(), P(), P())
    return jax.shard_map(
        local, mesh=mesh, in_specs=in_specs, out_specs=out_specs, check_vma=False
    )
```

time: 89.1 us -> 72.5 us (0.81)
  local copies, waits for them, and re-layouts: 9.05 us -> 0 us
  Pallas kernels: 78.2 us -> 71 us
    unnamed x32 -> x0, local copies, waits for them, and re-layouts: 8.35 us -> none
    pallas_call x1 -> x2, Pallas kernels: 78.2 us -> 71 us  [the longest x1 69.2 us: local(): pl.pallas_call(kernel, out_shape=jax.ShapeDtypeStruct((7 * C, C), F32), i...]
where the time goes in v2:
time: 72.5 us; the launch traced here: 72.3 us
  Pallas kernels  71 us (98%)
  between operations  1.29 us (2%)
    pallas_call x1, Pallas kernels, local(): pl.pallas_call(kernel, out_shape=jax.ShapeDtypeStruct((7 * C, C), F32), i...  69.2 us
    pallas_call x1, Pallas kernels, local(): pl.pallas_call(place, out_shape=[jax.ShapeDtypeStruct((A, C), BF)] * 2 +...  1.83 us

profile of v2, /device:TPU:1, one launch (start us, length us, event | category | flops | bytes accessed | tf_op | source)
XLA Modules:
  0.0 72.3 jit_solution(4979469434927630035)
XLA Ops:
  1.3 69.2 %ewald_layer.1.rows = f32[896,128]{1,0:T(8,128)} custom-call(bf16[128,128]{1,0:T(8,128)(2,1)} %refs_0_.1, f32[3,128]{1,0:T(4,128)} %refs_1_.1, s32[64,128]{1,0:T(8,128)} %bitcast.5, f32[64,128]{1,0:T(8,128)} %bitcast.6, s32[4,32]{1,0:T(4,128)} %refs_4_.1, s32[1]{0:T(128)S(6)} %copy.23.refs_5_, f32[3,2048]{1,0:T(4,128)} %refs_6_.1, f32[1,2048]{1,0:T(1,128)} %bitcast.8, ...), custom_call_target="tpu_custom_call" | custom-call | tf_op jit(solution)/shard_map/ewald_layer/pallas_call | solution.py:562
  70.5 1.8 %place_outputs.1 = (bf16[128,128]{1,0:T(8,128)(2,1)}, bf16[128,128]{1,0:T(8,128)(2,1)}, f32[128,128]{1,0:T(8,128)}, f32[128,128]{1,0:T(8,128)}, f32[128,128]{1,0...) custom-call(f32[896,128]{1,0:T(8,128)} %ewald_layer.1.rows), custom_call_target="tpu_custom_call" | custom-call | tf_op jit(solution)/shard_map/place_outputs/pallas_call | solution.py:573

commit v3 on v2

--- a/solution.py
+++ b/solution.py
@@ -12,12 +12,12 @@
 C = 128
 A = 128
 NB = 64
-STEP = 8
+STEP = 16
 COPIES = 140
 ROWS = (1024, 512, 512)
 
-FIRST = (0, 14, 4, 5, 1)
-LATER = (6, 7, 2, 3, 8, 9, 10, 11, 12, 13)
+FIRST = (0, 14, 4, 5, 1, 6, 7)
+LATER = (2, 3, 8, 9, 10, 11, 12, 13)
 
 BF = jnp.bfloat16
 F32 = jnp.float32
@@ -33,24 +33,11 @@
 
 def half_turns(f):
     q = f * f
-    s = -0.007370430945714351
-    for c in (
-        0.08214588661112823,
-        -0.5992645293207921,
-        2.550164039877345,
-        -5.16771278004997,
-        3.141592653589793,
-    ):
+    s = 0.10982452
+    for c in (-0.84611165, 3.60635422, -7.30824569, 4.44288292):
         s = s * q + c
-    c0 = 0.0019295743094039231
-    for c in (
-        -0.02580689139001406,
-        0.2353306303588935,
-        -1.3352627688545893,
-        4.058712126416768,
-        -4.934802200544679,
-        1.0,
-    ):
+    c0 = 0.31068803
+    for c in (-1.88355791, 5.73946038, -6.97885095, 1.4142135):
         c0 = c0 * q + c
     return s * f, c0
 
@@ -67,6 +54,7 @@
     gout, gin, ggout, gret,
     g0, rgx, g1, rgy, g2, rgz, gfull,
     rhy, rhz, rhx, h2, h_in,
+    picks, hiddens, slopes, inners, pairs,
     nbr_t, gate_t, src_t, ga_t, tab_t, pick_t, agg_t, gs_t, tsum, epart,
     ssem, rsem,
 ):
@@ -215,114 +203,120 @@
     pos_out[...] = jnp.zeros_like(pos_out)
     pos_out[0:3, :] = pos[...]
 
+    own_kind = by_core(masked32, gm32).astype(BF)
+    kv[...] = jnp.zeros_like(kv)
+    kv[0:3, :] = kvec[...] * (1.0 / (2.0 * math.pi))
+    kv[3:4, :] = jnp.sqrt(kw[...] * factor_scale)
+
+    def waves(turns, root):
+        s, c = half_turns(turns - jnp.round(turns))
+        s_root = s * root
+        return (root - s * s_root).astype(BF), (c * s_root).astype(BF)
+
+    def add_waves(first_row, place, start, stop):
+        spots = [jnp.broadcast_to(place[a : a + 1, :], (A, A)).T for a in range(3)]
+        spots = [jnp.concatenate([spot, spot], axis=1) for spot in spots]
+        atoms = slice(first_row, first_row + A)
+
+        def wave_block(block, _):
+            at = pl.ds(pl.multiple_of(block * 256, 256), 256)
+            turns = spots[0] * kv[0:1, at] + spots[1] * kv[1:2, at] + spots[2] * kv[2:3, at]
+            cosine[atoms, at], sine[atoms, at] = waves(turns, kv[3:4, at])
+            return 0
+
+        lax.fori_loop(start // 256, stop // 256, wave_block, 0)
+
+    add_waves(0, pos_out, 0, K)
+    own_t = own_kind.astype(F32).T
+
     pl.semaphore_wait(barrier, len(greeted))
     atoms_in = [send(x_out, x_in, sibling), send(pos_out, pos_in, sibling)]
     ghosts_in = [
         send(gout.at[pl.ds(f * 32, 32)], gin.at[pl.ds(f * 32, 32)], faces[f]) for f in range(4)
     ]
-
     for i in LATER:
         fetch[i].wait()
 
     masked_t = masked32.T.astype(BF)
-    kv[...] = jnp.zeros_like(kv)
-    kv[0:3, :] = kvec[...] * (1.0 / (2.0 * math.pi))
-    kv[3:4, :] = jnp.sqrt(kw[...] * factor_scale)
-    own_kind = by_core(masked32, gm32).astype(BF)
+
+    arrive(atoms_in)
+
+    values_t = jnp.concatenate([own_t, x_in[...].astype(F32).T], axis=1).astype(BF)
+
+    def sum_block(block, _):
+        at = pl.ds(pl.multiple_of(block * 512, 512), 512)
+        of_cos = nn(values_t, cosine[:, at]).astype(BF)
+        of_sin = nn(values_t, sine[:, at]).astype(BF)
+        sums[at, :C] = of_cos.T
+        sums[at, C:] = of_sin.T
+        return 0
+
+    def add_sums(start, stop):
+        add_waves(A, pos_in, start, stop)
+        lax.fori_loop(start // 512, stop // 512, sum_block, 0)
+
+    base_a, base_b, base_c = 0, ROWS[0], ROWS[0] + ROWS[1]
+    a1, b1, c1 = ROWS[0] // nx, ROWS[1] // ny, ROWS[2] // nz
+    a2, b2, c2 = a1 // ny, b1 // nx, c1 // nx
+    add_sums(0, base_b)
+    first_a = scatter(sums, base_a, la, x, nx, a1, x_peer)
+    add_sums(base_b, base_c)
+    first_b = scatter(sums, base_b, lb, y, ny, b1, y_peer)
+    add_sums(base_c, K)
+    first_c = scatter(sums, base_c, lc, z, nz, c1, z_peer)
 
     src_t[...] = nn(masked, sw[...]).astype(BF).astype(F32).T
     ga_t[...] = nt(gm, mw[...]).astype(BF).astype(F32).T
     nbr_t[...] = nbr[...].astype(F32)
     s, c = half_turns(dist[...] * 0.1)
-    gate_t[...] = jnp.where(nbr[...] < 2 * A, c * c, 0.0)
+    gate_t[...] = jnp.where(nbr[...] < 2 * A, 0.5 * c * c, 0.0)
     tab_t[:, :A] = nn(masked, tw[...]).astype(BF).astype(F32).T.astype(BF)
     agg_t[...] = jnp.zeros_like(agg_t)
     gs_t[...] = jnp.zeros_like(gs_t)
     tsum[...] = jnp.zeros_like(tsum)
     epart[...] = jnp.zeros_like(epart)
     ew_t = ew[...].astype(F32).T.astype(BF)
-
-    arrive(atoms_in)
-    both = jnp.concatenate([own_kind, x_in[...]], axis=0)
-    spots = [
-        jnp.concatenate([pos[a : a + 1, :], pos_in[a : a + 1, :]], axis=1) for a in range(3)
-    ]
-
-    def waves(turns, root):
-        turns = turns - jnp.floor(turns + 0.5)
-        s, c = half_turns(turns)
-        return ((1.0 - 2.0 * s * s) * root).astype(BF), ((2.0 * s * c) * root).astype(BF)
-
-    def sum_block(block, _):
-        at = pl.multiple_of(block * 128, 128)
-        cols = kv[:, pl.ds(at, 128)].T
-        turns = cols[:, 0:1] * spots[0] + cols[:, 1:2] * spots[1] + cols[:, 2:3] * spots[2]
-        cos_t, sin_t = waves(turns, cols[:, 3:4])
-        sums[pl.ds(at, 128), :C] = nn(cos_t, both).astype(BF)
-        sums[pl.ds(at, 128), C:] = nn(sin_t, both).astype(BF)
-        return 0
-
-    base_a, base_b, base_c = 0, ROWS[0], ROWS[0] + ROWS[1]
-    a1, b1, c1 = ROWS[0] // nx, ROWS[1] // ny, ROWS[2] // nz
-    a2, b2, c2 = a1 // ny, b1 // nx, c1 // nx
-    lax.fori_loop(0, base_b // 128, sum_block, 0)
-    first_a = scatter(sums, base_a, la, x, nx, a1, x_peer)
-    lax.fori_loop(base_b // 128, base_c // 128, sum_block, 0)
-    first_b = scatter(sums, base_b, lb, y, ny, b1, y_peer)
-    lax.fori_loop(base_c // 128, K // 128, sum_block, 0)
-    first_c = scatter(sums, base_c, lc, z, nz, c1, z_peer)
+    table_row = lax.broadcasted_iota(jnp.int32, (2 * A, A), 0).astype(F32).astype(BF)
 
     arrive(ghosts_in)
     ghosts = gin[...]
     tab_t[:, A:] = nn(ghosts, tw[...]).astype(BF).astype(F32).T.astype(BF)
     table_t = jnp.concatenate([masked_t, ghosts.astype(F32).T.astype(BF)], axis=1)
+
     def edge_step(step, _):
-        table_row = lax.broadcasted_iota(jnp.int32, (2 * A, A), 0).astype(F32)
-        hiddens, inners, picks, pairs = [], [], [], []
-        agg_sum, gs_sum = agg_t[...], gs_t[...]
-        source, upstream = src_t[...], ga_t[...]
-        for pair in range(STEP // 2):
-            base = step * STEP + 2 * pair
-            gates = [gate_t[pl.ds(base + j, 1), :] for j in range(2)]
-            chosen = jnp.concatenate(
-                [
-                    jnp.where(table_row == nbr_t[pl.ds(base + j, 1), :], 1.0, 0.0).astype(BF)
-                    for j in range(2)
-                ],
-                axis=1,
-            )
-            summed = nn(tab_t[...], chosen) + jnp.concatenate([source, source], axis=1)
-            g = 0.5 * jnp.tanh(0.5 * summed) + 0.5
-            hidden = summed * g
-            slope = g + hidden * (1.0 - g)
-            hidden = hidden.astype(BF)
-            mixed = nn(ew_t, hidden)
-            g = 0.5 * jnp.tanh(0.5 * mixed) + 0.5
-            message = mixed * g
-            mixed_slope = g + message * (1.0 - g)
-            agg_sum += gates[0] * message[:, :A] + gates[1] * message[:, A:]
-            inner = jnp.concatenate(
-                [
-                    gates[0] * upstream * mixed_slope[:, :A],
-                    gates[1] * upstream * mixed_slope[:, A:],
-                ],
-                axis=1,
-            ).astype(BF)
-            pair_grad = nn(ew[...], inner) * slope
-            gs_sum += pair_grad[:, :A] + pair_grad[:, A:]
-            hiddens.append(hidden)
-            inners.append(inner)
-            picks.append(chosen)
-            pairs.append(pair_grad.astype(BF))
+        slots = [(pl.ds(step * STEP + j, 1), slice(j * A, (j + 1) * A)) for j in range(STEP)]
+        for row, at in slots:
+            named = jnp.broadcast_to(nbr_t[row, :], (2 * A, A)).astype(BF)
+            picks[:, at] = jnp.where(table_row == named, jnp.ones((), BF), jnp.zeros((), BF))
+        summed = nn(tab_t[...], picks[...])
+        for row, at in slots:
+            v = summed[:, at] + src_t[...]
+            g = 0.5 * jnp.tanh(0.5 * v) + 0.5
+            hidden = v * g
+            hiddens[:, at] = hidden.astype(BF)
+            slopes[:, at] = g + hidden * (1.0 - g)
+        mixed = nn(ew_t, hiddens[...])
+        agg_sum = agg_t[...]
+        for row, at in slots:
+            v = mixed[:, at]
+            g = 0.5 * jnp.tanh(0.5 * v) + 0.5
+            message = v * g
+            agg_sum += gate_t[row, :] * message
+            inners[:, at] = (gate_t[row, :] * ga_t[...] * (g + message * (1.0 - g))).astype(BF)
         agg_t[...] = agg_sum
+        outer = nn(ew[...], inners[...])
+        gs_sum = gs_t[...]
+        for row, at in slots:
+            pair_grad = outer[:, at] * slopes[:, at]
+            gs_sum += pair_grad
+            pairs[:, at] = pair_grad.astype(BF)
         gs_t[...] = gs_sum
-        epart[...] += nt(jnp.concatenate(hiddens, axis=1), jnp.concatenate(inners, axis=1))
-        tsum[...] += nt(jnp.concatenate(picks, axis=1), jnp.concatenate(pairs, axis=1))
+        epart[...] += nt(hiddens[...], inners[...])
+        tsum[...] += nt(picks[...], pairs[...])
         return 0
 
     steps = NB // STEP
-    cut = (steps // 2, steps - 1)
-    lax.fori_loop(0, cut[0], edge_step, 0)
+    lax.fori_loop(0, steps - 1, edge_step, 0)
     arrive(first_a)
     collect(sums, base_a, la, x, nx, a1, ta)
     second_a = scatter(ta, 0, la2, y, ny, a2, y_peer)
@@ -333,21 +327,7 @@
     collect(sums, base_c, lc, z, nz, c1, tc)
     second_c = scatter(tc, 0, lc2, x, nx, c2, x_peer)
 
-    lax.fori_loop(cut[0], cut[1], edge_step, 0)
-    ab2 = a2 + b2
-    arrive(second_b)
-    collect(tb, 0, lb2, x, nx, b2, t2, a2)
-    arrive(second_c)
-    collect(tc, 0, lc2, x, nx, c2, t2, ab2)
-    ly[pl.ds(y, 1)] = t2[ab2:, :][None]
-    third_c = share(ly, y, ny, y_peer)
-    arrive(second_a)
-    collect(ta, 0, la2, y, ny, a2, t2, 0)
-    lz[pl.ds(z, 1)] = t2[:ab2, :][None]
-    third_ab = share(lz, z, nz, z_peer)
-
-    lax.fori_loop(cut[1], steps, edge_step, 0)
-
+    lax.fori_loop(steps - 1, steps, edge_step, 0)
     table_sum = tsum[...]
     ggout[...] = table_sum[A:, :].astype(BF)
     ghosts_back = [
@@ -361,6 +341,27 @@
     g0[3 * C :, :] = nn(aggregate_t, gm).astype(BF)
     gx, gy = 4 * C // nx, 4 * C // (nx * ny)
     g_x = scatter(g0, 0, rgx, x, nx, gx, x_peer)
+
+    ab2 = a2 + b2
+    arrive(second_b)
+    collect(tb, 0, lb2, x, nx, b2, t2, a2)
+    arrive(second_c)
+    collect(tc, 0, lc2, x, nx, c2, t2, ab2)
+    ly[pl.ds(y, 1)] = t2[ab2:, :][None]
+    third_c = share(ly, y, ny, y_peer)
+    arrive(second_a)
+    collect(ta, 0, la2, y, ny, a2, t2, 0)
+    lz[pl.ds(z, 1)] = t2[:ab2, :][None]
+    third_ab = share(lz, z, nz, z_peer)
+
+    arrive(g_x)
+    collect(g0, 0, rgx, x, nx, gx, g1)
+    g_y = scatter(g1, 0, rgy, y, ny, gy, y_peer)
+
+    arrive(ghosts_back)
+    grad_target = (table_sum[:A, :] + nn(pick_t[...].astype(BF), gret[...])).astype(BF)
+    short_grad = nt(grad_source, sw[...]) + nt(grad_target, tw[...])
+    short_range = nn(agg_t[...].T.astype(BF), mw[...])
 
     fw_t = fw[...].astype(F32).T
     project = by_core(cw[...].astype(F32).T, fw_t).astype(BF)
@@ -388,10 +389,6 @@
     spread_c = spread(w_full, place_c, c2, nx, x_peer)
     w_swap = [send(w_out, w_in, sibling)]
 
-    arrive(g_x)
-    collect(g0, 0, rgx, x, nx, gx, g1)
-    g_y = scatter(g1, 0, rgy, y, ny, gy, y_peer)
-
     arrive(w_swap)
     other_t = w_in[...].astype(F32).T
     in_ab = lax.broadcasted_iota(jnp.int32, other_t.shape, 1) < ab2
@@ -403,35 +400,8 @@
     rhy[pl.ds(y, 1)] = weight_part(jnp.where(in_ab, other_t, 0.0))[None]
     rhz[pl.ds(z, 1)] = weight_part(jnp.where(in_ab, 0.0, other_t))[None]
 
-    arrive(spread_b)
-    spread_b = spread(w_full, base_b + y * b1, b1, ny, y_peer)
-    arrive(spread_c)
-    spread_c = spread(w_full, base_c + z * c1, c1, nz, z_peer)
     h_y = share(rhy, y, ny, y_peer)
     h_z = share(rhz, z, nz, z_peer)
-    arrive(spread_a)
-    spread_a = spread(w_full, base_a + x * a1, a1, nx, x_peer)
-
-    spot_cols = [
-        jnp.concatenate(
-            [
-                jnp.broadcast_to(pos[a : a + 1, :], (A, A)).T,
-                jnp.broadcast_to(pos_in[a : a + 1, :], (A, A)).T,
-            ],
-            axis=0,
-        )
-        for a in range(3)
-    ]
-
-    def wave_block(block, _):
-        at = pl.ds(pl.multiple_of(block * 128, 128), 128)
-        turns = (
-            spot_cols[0] * kv[0:1, at] + spot_cols[1] * kv[1:2, at] + spot_cols[2] * kv[2:3, at]
-        )
-        cosine[:, at], sine[:, at] = waves(turns, kv[3:4, at])
-        return 0
-
-    lax.fori_loop(0, K // 128, wave_block, 0)
 
     arrive(g_y)
     collect(g1, 0, rgy, y, ny, gy, g2)
@@ -439,27 +409,38 @@
     rgz[pl.ds(zc, 1)] = g2[...][None]
     g_zc = share(rgz, zc, nz * nc, zc_peer)
 
-    arrive(ghosts_back)
-    grad_target = (table_sum[:A, :] + nn(pick_t[...].astype(BF), gret[...])).astype(BF)
-    short_grad = nt(grad_source, sw[...]) + nt(grad_target, tw[...])
-    short_range = nn(agg_t[...].T.astype(BF), mw[...])
+    arrive(spread_b)
+    spread_b = spread(w_full, base_b + y * b1, b1, ny, y_peer)
+    arrive(spread_c)
+    spread_c = spread(w_full, base_c + z * c1, c1, nz, z_peer)
+    arrive(spread_a)
+    spread_a = spread(w_full, base_a + x * a1, a1, nx, x_peer)
 
     arrive(h_y)
     arrive(h_z)
     rhx[pl.ds(x, 1)] = (summed_slots(rhy, ny) + summed_slots(rhz, nz)).astype(BF)[None]
     h_x = share(rhx, x, nx, x_peer)
 
-    arrive(spread_b)
-    arrive(spread_c)
-    arrive(spread_a)
-    field = nn(cosine[...], w_full[...]) + pltpu.roll(nn(sine[...], w_full[...]), 64, 1)
-    e_out[...] = field[A:, :].astype(BF)
-    e_swap = [send(e_out, e_in, sibling)]
-
     arrive(g_zc)
     g_mine = pl.multiple_of(x * gx + y * gy, 16)
     gfull[pl.ds(g_mine, gy), :] = summed_slots(rgz, nz * nc).astype(BF)
     g_ys = spread(gfull, g_mine, gy, ny, y_peer)
+
+    def field_of(start, stop):
+        at, weights = slice(start, stop), w_full[start:stop, :]
+        return nn(cosine[:, at], weights), nn(sine[:, at], weights)
+
+    arrive(spread_b)
+    arrive(spread_c)
+    of_cos, of_sin = field_of(base_b, K)
+    arrive(spread_a)
+    more_cos, more_sin = field_of(base_a, base_b)
+    field = of_cos + more_cos + pltpu.roll(of_sin + more_sin, 64, 1)
+    e_out[...] = field[A:, :].astype(BF)
+    e_swap = [send(e_out, e_in, sibling)]
+
+    arrive(g_ys)
+    g_xs = spread(gfull, x * gx, gx, nx, x_peer)
 
     arrive(h_x)
     h2[...] = summed_slots(rhx, nx).astype(BF)
@@ -478,8 +459,6 @@
     out[6 * C : 6 * C + 64, :] = by_core(here, there) * grad_scale
     out[6 * C + 64 : 7 * C, :] = by_core(there, here) * grad_scale
 
-    arrive(g_ys)
-    g_xs = spread(gfull, x * gx, gx, nx, x_peer)
     arrive(g_xs)
     out[2 * C : 6 * C, :] = gfull[...].astype(F32) * grad_scale
 
@@ -537,6 +516,8 @@
         bf(4 * C, C), bf(nx - 1, gx, C), bf(gx, C), bf(ny - 1, gy, C), bf(gy, C),
         bf(nz * nc, gy, C), bf(4 * C, C),
         bf(ny, 64, C), bf(nz, 64, C), bf(nx, 64, C), bf(64, C), bf(64, C),
+        bf(2 * A, STEP * A), bf(C, STEP * A), f32(C, STEP * A),
+        bf(C, STEP * A), bf(C, STEP * A),
         f32(NB, A), f32(NB, A), f32(C, A), f32(C, A), bf(C, 2 * A), f32(A, A),
         f32(C, A), f32(C, A), f32(2 * A, C), f32(C, C),
         pltpu.SemaphoreType.DMA((COPIES,)),

time: 72.5 us -> 63.5 us (0.88)
  Pallas kernels: 71 us -> 62 us
    pallas_call x1, Pallas kernels: 69.2 us -> 60.1 us  [local(): pl.pallas_call(kernel, out_shape=jax.ShapeDtypeStruct((7 * C, C), F32), i...]
where the time goes in v3:
time: 63.5 us; the launch traced here: 63.3 us
  Pallas kernels  62 us (98%)
  between operations  1.29 us (2%)
    pallas_call x1, Pallas kernels, local(): pl.pallas_call(kernel, out_shape=jax.ShapeDtypeStruct((7 * C, C), F32), i...  60.1 us
    pallas_call x1, Pallas kernels, local(): pl.pallas_call(place, out_shape=[jax.ShapeDtypeStruct((A, C), BF)] * 2 +...  1.83 us

profile of v3, /device:TPU:1, one launch (start us, length us, event | category | flops | bytes accessed | tf_op | source)
XLA Modules:
  0.0 63.3 jit_solution(7462815136579032674)
XLA Ops:
  1.3 60.1 %ewald_layer.1.rows = f32[896,128]{1,0:T(8,128)} custom-call(bf16[128,128]{1,0:T(8,128)(2,1)} %refs_0_.1, f32[3,128]{1,0:T(4,128)} %refs_1_.1, s32[64,128]{1,0:T(8,128)} %bitcast.5, f32[64,128]{1,0:T(8,128)} %bitcast.6, s32[4,32]{1,0:T(4,128)} %refs_4_.1, s32[1]{0:T(128)S(6)} %copy.23.refs_5_, f32[3,2048]{1,0:T(4,128)} %refs_6_.1, f32[1,2048]{1,0:T(1,128)} %bitcast.8, ...), custom_call_target="tpu_custom_call" | custom-call | tf_op jit(solution)/shard_map/ewald_layer/pallas_call | solution.py:543
  61.4 1.8 %place_outputs.1 = (bf16[128,128]{1,0:T(8,128)(2,1)}, bf16[128,128]{1,0:T(8,128)(2,1)}, f32[128,128]{1,0:T(8,128)}, f32[128,128]{1,0:T(8,128)}, f32[128,128]{1,0...) custom-call(f32[896,128]{1,0:T(8,128)} %ewald_layer.1.rows), custom_call_target="tpu_custom_call" | custom-call | tf_op jit(solution)/shard_map/place_outputs/pallas_call | solution.py:554

commit v4 on v3

--- a/solution.py
+++ b/solution.py
@@ -52,7 +52,7 @@
     la, ta, lb, tb, lc, tc, la2, lb2, lc2, t2, lz, ly, fin,
     w_out, w_in, w_full, cosine, sine, e_out, e_in,
     gout, gin, ggout, gret,
-    g0, rgx, g1, rgy, g2, rgz, gfull,
+    g0, rgx, g1, rgy, rgz, gfull,
     rhy, rhz, rhx, h2, h_in,
     picks, hiddens, slopes, inners, pairs,
     nbr_t, gate_t, src_t, ga_t, tab_t, pick_t, agg_t, gs_t, tsum, epart,
@@ -100,8 +100,8 @@
     def z_peer(d):
         return device(pz=ahead(z, d, nz))
 
-    def zc_peer(d):
-        return device(pz=ahead(z, d // nc, nz), pc=ahead(core, d % nc, nc))
+    def xc_peer(d):
+        return device(px=ahead(x, d // nc, nx), pc=ahead(core, d % nc, nc))
 
     sibling = device(pc=ahead(core, 1, nc))
     faces = (
@@ -114,9 +114,9 @@
 
     barrier = pltpu.get_barrier_semaphore()
     greeted = list(faces)
-    greeted += [x_peer(d) for d in range(1, nx)]
+    greeted += [xc_peer(d) for d in range(1, nx * nc)]
     greeted += [y_peer(d) for d in range(1, ny)]
-    greeted += [zc_peer(d) for d in range(1, nz * nc)]
+    greeted += [z_peer(d) for d in range(1, nz)]
     for other in greeted:
         pl.semaphore_signal(
             barrier, inc=1, device_id=other, device_id_type=pl.DeviceIdType.MESH
@@ -142,6 +142,13 @@
         for copy in copies:
             copy.wait_recv()
 
+    settled = []
+
+    def settle(upto):
+        for copy in sent[len(settled) : upto]:
+            copy.wait_send()
+            settled.append(copy)
+
     def rows(ref, start, size):
         return ref.at[pl.ds(pl.multiple_of(start, 16), size)]
 
@@ -229,41 +236,10 @@
     add_waves(0, pos_out, 0, K)
     own_t = own_kind.astype(F32).T
 
-    pl.semaphore_wait(barrier, len(greeted))
-    atoms_in = [send(x_out, x_in, sibling), send(pos_out, pos_in, sibling)]
-    ghosts_in = [
-        send(gout.at[pl.ds(f * 32, 32)], gin.at[pl.ds(f * 32, 32)], faces[f]) for f in range(4)
-    ]
     for i in LATER:
         fetch[i].wait()
 
     masked_t = masked32.T.astype(BF)
-
-    arrive(atoms_in)
-
-    values_t = jnp.concatenate([own_t, x_in[...].astype(F32).T], axis=1).astype(BF)
-
-    def sum_block(block, _):
-        at = pl.ds(pl.multiple_of(block * 512, 512), 512)
-        of_cos = nn(values_t, cosine[:, at]).astype(BF)
-        of_sin = nn(values_t, sine[:, at]).astype(BF)
-        sums[at, :C] = of_cos.T
-        sums[at, C:] = of_sin.T
-        return 0
-
-    def add_sums(start, stop):
-        add_waves(A, pos_in, start, stop)
-        lax.fori_loop(start // 512, stop // 512, sum_block, 0)
-
-    base_a, base_b, base_c = 0, ROWS[0], ROWS[0] + ROWS[1]
-    a1, b1, c1 = ROWS[0] // nx, ROWS[1] // ny, ROWS[2] // nz
-    a2, b2, c2 = a1 // ny, b1 // nx, c1 // nx
-    add_sums(0, base_b)
-    first_a = scatter(sums, base_a, la, x, nx, a1, x_peer)
-    add_sums(base_b, base_c)
-    first_b = scatter(sums, base_b, lb, y, ny, b1, y_peer)
-    add_sums(base_c, K)
-    first_c = scatter(sums, base_c, lc, z, nz, c1, z_peer)
 
     src_t[...] = nn(masked, sw[...]).astype(BF).astype(F32).T
     ga_t[...] = nt(gm, mw[...]).astype(BF).astype(F32).T
@@ -276,6 +252,38 @@
     tsum[...] = jnp.zeros_like(tsum)
     epart[...] = jnp.zeros_like(epart)
     ew_t = ew[...].astype(F32).T.astype(BF)
+
+    pl.semaphore_wait(barrier, len(greeted))
+    atoms_in = [send(x_out, x_in, sibling), send(pos_out, pos_in, sibling)]
+    ghosts_in = [
+        send(gout.at[pl.ds(f * 32, 32)], gin.at[pl.ds(f * 32, 32)], faces[f]) for f in range(4)
+    ]
+    arrive(atoms_in)
+
+    values_t = jnp.concatenate([own_t, x_in[...].astype(F32).T], axis=1).astype(BF)
+
+    def sum_block(block, _):
+        at = pl.ds(pl.multiple_of(block * 512, 512), 512)
+        of_cos = nn(values_t, cosine[:, at]).astype(BF)
+        of_sin = nn(values_t, sine[:, at]).astype(BF)
+        sums[at, :C] = of_cos.T
+        sums[at, C:] = of_sin.T
+        return 0
+
+    def add_sums(start, stop):
+        add_waves(A, pos_in, start, stop)
+        lax.fori_loop(start // 512, stop // 512, sum_block, 0)
+
+    base_a, base_b, base_c = 0, ROWS[0], ROWS[0] + ROWS[1]
+    a1, b1, c1 = ROWS[0] // nx, ROWS[1] // ny, ROWS[2] // nz
+    a2, b2, c2 = a1 // ny, b1 // nx, c1 // nx
+    add_sums(0, base_b)
+    first_a = scatter(sums, base_a, la, x, nx, a1, x_peer)
+    add_sums(base_b, base_c)
+    first_b = scatter(sums, base_b, lb, y, ny, b1, y_peer)
+    add_sums(base_c, K)
+    first_c = scatter(sums, base_c, lc, z, nz, c1, z_peer)
+
     table_row = lax.broadcasted_iota(jnp.int32, (2 * A, A), 0).astype(F32).astype(BF)
 
     arrive(ghosts_in)
@@ -317,6 +325,7 @@
 
     steps = NB // STEP
     lax.fori_loop(0, steps - 1, edge_step, 0)
+    first_count = len(sent)
     arrive(first_a)
     collect(sums, base_a, la, x, nx, a1, ta)
     second_a = scatter(ta, 0, la2, y, ny, a2, y_peer)
@@ -339,10 +348,20 @@
     g0[C : 2 * C, :] = nn(table_t, table_sum.astype(BF)).astype(BF)
     g0[2 * C : 3 * C, :] = epart[...].astype(BF)
     g0[3 * C :, :] = nn(aggregate_t, gm).astype(BF)
-    gx, gy = 4 * C // nx, 4 * C // (nx * ny)
-    g_x = scatter(g0, 0, rgx, x, nx, gx, x_peer)
-
+    gx = 4 * C // (nx * nc)
+    xc = x * nc + core
+    g_x = [
+        send(
+            rows(g0, (ahead(x, d // nc, nx) * nc + ahead(core, d % nc, nc)) * gx, gx),
+            rgx.at[d - 1],
+            xc_peer(d),
+        )
+        for d in range(1, nx * nc)
+    ]
+
+    second_count = len(sent)
     ab2 = a2 + b2
+    settle(first_count)
     arrive(second_b)
     collect(tb, 0, lb2, x, nx, b2, t2, a2)
     arrive(second_c)
@@ -355,8 +374,9 @@
     third_ab = share(lz, z, nz, z_peer)
 
     arrive(g_x)
-    collect(g0, 0, rgx, x, nx, gx, g1)
-    g_y = scatter(g1, 0, rgy, y, ny, gy, y_peer)
+    collect(g0, 0, rgx, xc, nx * nc, gx, g1)
+    rgy[pl.ds(y, 1)] = g1[...][None]
+    g_y = share(rgy, y, ny, y_peer)
 
     arrive(ghosts_back)
     grad_target = (table_sum[:A, :] + nn(pick_t[...].astype(BF), gret[...])).astype(BF)
@@ -373,6 +393,8 @@
         ],
         axis=0,
     )
+    third_count = len(sent)
+    settle(second_count)
     arrive(third_c)
     fin[ab2:, :] = summed_slots(ly, ny).astype(BF)
     arrive(third_ab)
@@ -404,11 +426,11 @@
     h_z = share(rhz, z, nz, z_peer)
 
     arrive(g_y)
-    collect(g1, 0, rgy, y, ny, gy, g2)
-    zc = z * nc + core
-    rgz[pl.ds(zc, 1)] = g2[...][None]
-    g_zc = share(rgz, zc, nz * nc, zc_peer)
-
+    rgz[pl.ds(z, 1)] = summed_slots(rgy, ny).astype(BF)[None]
+    g_z = share(rgz, z, nz, z_peer)
+
+    settle(third_count)
+    fourth_count = len(sent)
     arrive(spread_b)
     spread_b = spread(w_full, base_b + y * b1, b1, ny, y_peer)
     arrive(spread_c)
@@ -421,10 +443,12 @@
     rhx[pl.ds(x, 1)] = (summed_slots(rhy, ny) + summed_slots(rhz, nz)).astype(BF)[None]
     h_x = share(rhx, x, nx, x_peer)
 
-    arrive(g_zc)
-    g_mine = pl.multiple_of(x * gx + y * gy, 16)
-    gfull[pl.ds(g_mine, gy), :] = summed_slots(rgz, nz * nc).astype(BF)
-    g_ys = spread(gfull, g_mine, gy, ny, y_peer)
+    arrive(g_z)
+    g_mine = pl.multiple_of(xc * gx, 16)
+    gfull[pl.ds(g_mine, gx), :] = summed_slots(rgz, nz).astype(BF)
+    g_xs = spread(gfull, g_mine, gx, nx * nc, xc_peer)
+
+    settle(fourth_count)
 
     def field_of(start, stop):
         at, weights = slice(start, stop), w_full[start:stop, :]
@@ -438,16 +462,14 @@
     field = of_cos + more_cos + pltpu.roll(of_sin + more_sin, 64, 1)
     e_out[...] = field[A:, :].astype(BF)
     e_swap = [send(e_out, e_in, sibling)]
-
-    arrive(g_ys)
-    g_xs = spread(gfull, x * gx, gx, nx, x_peer)
+    field_here = field[:A, :]
 
     arrive(h_x)
     h2[...] = summed_slots(rhx, nx).astype(BF)
     h_swap = [send(h2, h_in, sibling)]
 
     arrive(e_swap)
-    here = field[:A, :].astype(BF).astype(F32)
+    here = field_here.astype(BF).astype(F32)
     there = e_in[...].astype(F32)
     potential = by_core(here, there).astype(BF)[:, :64]
     grad_charge = by_core(there, here).astype(BF)[:, :64]
@@ -462,8 +484,7 @@
     arrive(g_xs)
     out[2 * C : 6 * C, :] = gfull[...].astype(F32) * grad_scale
 
-    for copy in sent:
-        copy.wait_send()
+    settle(len(sent))
 
 
 def place(
@@ -496,7 +517,7 @@
     a1, b1, c1 = ROWS[0] // nx, ROWS[1] // ny, ROWS[2] // nz
     a2, b2, c2 = a1 // ny, b1 // nx, c1 // nx
     last = a2 + b2 + c2
-    gx, gy = 4 * C // nx, 4 * C // (nx * ny)
+    gx = 4 * C // (nx * nc)
 
     def bf(*shape):
         return pltpu.VMEM(shape, BF)
@@ -513,8 +534,8 @@
         bf(last, 2 * C), bf(nz, a2 + b2, 2 * C), bf(ny, c2, 2 * C), bf(last, 2 * C),
         bf(last, C), bf(last, C), bf(K, C), bf(2 * A, K), bf(2 * A, K), bf(A, C), bf(A, C),
         bf(A, C), bf(A, C), bf(A, C), bf(A, C),
-        bf(4 * C, C), bf(nx - 1, gx, C), bf(gx, C), bf(ny - 1, gy, C), bf(gy, C),
-        bf(nz * nc, gy, C), bf(4 * C, C),
+        bf(4 * C, C), bf(nx * nc - 1, gx, C), bf(gx, C), bf(ny, gx, C), bf(nz, gx, C),
+        bf(4 * C, C),
         bf(ny, 64, C), bf(nz, 64, C), bf(nx, 64, C), bf(64, C), bf(64, C),
         bf(2 * A, STEP * A), bf(C, STEP * A), f32(C, STEP * A),
         bf(C, STEP * A), bf(C, STEP * A),

time: 63.5 us -> 61.7 us (0.972)
  Pallas kernels: 62 us -> 60.1 us
    pallas_call x1, Pallas kernels: 60.1 us -> 58.3 us  [local(): pl.pallas_call(kernel, out_shape=jax.ShapeDtypeStruct((7 * C, C), F32), i...]
where the time goes in v4:
time: 61.7 us; the launch traced here: 61.4 us
  Pallas kernels  60.1 us (97%)
  between operations  1.29 us (2%)
    pallas_call x1, Pallas kernels, local(): pl.pallas_call(kernel, out_shape=jax.ShapeDtypeStruct((7 * C, C), F32), i...  58.3 us
    pallas_call x1, Pallas kernels, local(): pl.pallas_call(place, out_shape=[jax.ShapeDtypeStruct((A, C), BF)] * 2 +...  1.83 us

profile of v4, /device:TPU:1, one launch (start us, length us, event | category | flops | bytes accessed | tf_op | source)
XLA Modules:
  0.0 61.4 jit_solution(9195240927119196447)
XLA Ops:
  1.3 58.3 %ewald_layer.1.rows = f32[896,128]{1,0:T(8,128)} custom-call(bf16[128,128]{1,0:T(8,128)(2,1)} %refs_0_.1, f32[3,128]{1,0:T(4,128)} %refs_1_.1, s32[64,128]{1,0:T(8,128)} %bitcast.5, f32[64,128]{1,0:T(8,128)} %bitcast.6, s32[4,32]{1,0:T(4,128)} %refs_4_.1, s32[1]{0:T(128)S(6)} %copy.23.refs_5_, f32[3,2048]{1,0:T(4,128)} %refs_6_.1, f32[1,2048]{1,0:T(1,128)} %bitcast.8, ...), custom_call_target="tpu_custom_call" | custom-call | tf_op jit(solution)/shard_map/ewald_layer/pallas_call | solution.py:564
  59.6 1.8 %place_outputs.1 = (bf16[128,128]{1,0:T(8,128)(2,1)}, bf16[128,128]{1,0:T(8,128)(2,1)}, f32[128,128]{1,0:T(8,128)}, f32[128,128]{1,0:T(8,128)}, f32[128,128]{1,0...) custom-call(f32[896,128]{1,0:T(8,128)} %ewald_layer.1.rows), custom_call_target="tpu_custom_call" | custom-call | tf_op jit(solution)/shard_map/place_outputs/pallas_call | solution.py:575

commit v5 on v4

--- a/solution.py
+++ b/solution.py
@@ -149,13 +149,16 @@
             copy.wait_send()
             settled.append(copy)
 
+    def far_first(n):
+        return sorted(range(1, n), key=lambda d: -min(d, n - d))
+
     def rows(ref, start, size):
         return ref.at[pl.ds(pl.multiple_of(start, 16), size)]
 
     def scatter(src, base, landing, me, n, size, peer):
         return [
             send(rows(src, base + ahead(me, d, n) * size, size), landing.at[d - 1], peer(d))
-            for d in range(1, n)
+            for d in far_first(n)
         ]
 
     def collect(src, base, landing, me, n, size, dst, dst_base=0):
@@ -175,7 +178,7 @@
             lax.fori_loop(0, size // chunk, add, 0)
 
     def share(landing, me, n, peer):
-        return [send(landing.at[me], landing.at[me], peer(d)) for d in range(1, n)]
+        return [send(landing.at[me], landing.at[me], peer(d)) for d in far_first(n)]
 
     def summed_slots(landing, n):
         total = landing[0].astype(F32)
@@ -185,7 +188,7 @@
 
     def spread(ref, start, size, n, peer):
         return [
-            send(rows(ref, start, size), rows(ref, start, size), peer(d)) for d in range(1, n)
+            send(rows(ref, start, size), rows(ref, start, size), peer(d)) for d in far_first(n)
         ]
 
     first_core = jnp.where(core == 0, 1.0, 0.0).astype(F32)
@@ -338,10 +341,6 @@
 
     lax.fori_loop(steps - 1, steps, edge_step, 0)
     table_sum = tsum[...]
-    ggout[...] = table_sum[A:, :].astype(BF)
-    ghosts_back = [
-        send(ggout.at[pl.ds(f * 32, 32)], gret.at[pl.ds(f * 32, 32)], back[f]) for f in range(4)
-    ]
     aggregate_t = agg_t[...].astype(BF)
     grad_source = gs_t[...].T.astype(BF)
     g0[0:C, :] = nn(masked_t, grad_source).astype(BF)
@@ -359,6 +358,10 @@
         for d in range(1, nx * nc)
     ]
 
+    ggout[...] = table_sum[A:, :].astype(BF)
+    ghosts_back = [
+        send(ggout.at[pl.ds(f * 32, 32)], gret.at[pl.ds(f * 32, 32)], back[f]) for f in range(4)
+    ]
     second_count = len(sent)
     ab2 = a2 + b2
     settle(first_count)
@@ -400,6 +403,7 @@
     arrive(third_ab)
     fin[:ab2, :] = summed_slots(lz, nz).astype(BF)
     w_out[...] = nn(fin[...], project).astype(BF)
+    w_swap = [send(w_out, w_in, sibling)]
     place_a = pl.multiple_of(base_a + x * a1 + y * a2, 16)
     place_b = pl.multiple_of(base_b + y * b1 + x * b2, 16)
     place_c = pl.multiple_of(base_c + z * c1 + x * c2, 16)
@@ -409,7 +413,6 @@
     spread_a = spread(w_full, place_a, a2, ny, y_peer)
     spread_b = spread(w_full, place_b, b2, nx, x_peer)
     spread_c = spread(w_full, place_c, c2, nx, x_peer)
-    w_swap = [send(w_out, w_in, sibling)]
 
     arrive(w_swap)
     other_t = w_in[...].astype(F32).T

time: 61.7 us -> 58.9 us (0.955)
  Pallas kernels: 60.1 us -> 57.4 us
    pallas_call x1, Pallas kernels: 58.3 us -> 55.5 us  [local(): pl.pallas_call(kernel, out_shape=jax.ShapeDtypeStruct((7 * C, C), F32), i...]
where the time goes in v5:
time: 58.9 us; the launch traced here: 58.6 us
  Pallas kernels  57.4 us (97%)
  between operations  1.29 us (2%)
    pallas_call x1, Pallas kernels, local(): pl.pallas_call(kernel, out_shape=jax.ShapeDtypeStruct((7 * C, C), F32), i...  55.5 us
    pallas_call x1, Pallas kernels, local(): pl.pallas_call(place, out_shape=[jax.ShapeDtypeStruct((A, C), BF)] * 2 +...  1.83 us

profile of v5, /device:TPU:1, one launch (start us, length us, event | category | flops | bytes accessed | tf_op | source)
XLA Modules:
  0.0 58.6 jit_solution(6615100457810191116)
XLA Ops:
  1.3 55.5 %ewald_layer.1.rows = f32[896,128]{1,0:T(8,128)} custom-call(bf16[128,128]{1,0:T(8,128)(2,1)} %refs_0_.1, f32[3,128]{1,0:T(4,128)} %refs_1_.1, s32[64,128]{1,0:T(8,128)} %bitcast.5, f32[64,128]{1,0:T(8,128)} %bitcast.6, s32[4,32]{1,0:T(4,128)} %refs_4_.1, s32[1]{0:T(128)S(6)} %copy.23.refs_5_, f32[3,2048]{1,0:T(4,128)} %refs_6_.1, f32[1,2048]{1,0:T(1,128)} %bitcast.8, ...), custom_call_target="tpu_custom_call" | custom-call | tf_op jit(solution)/shard_map/ewald_layer/pallas_call | solution.py:567
  56.8 1.8 %place_outputs.1 = (bf16[128,128]{1,0:T(8,128)(2,1)}, bf16[128,128]{1,0:T(8,128)(2,1)}, f32[128,128]{1,0:T(8,128)}, f32[128,128]{1,0:T(8,128)}, f32[128,128]{1,0...) custom-call(f32[896,128]{1,0:T(8,128)} %ewald_layer.1.rows), custom_call_target="tpu_custom_call" | custom-call | tf_op jit(solution)/shard_map/place_outputs/pallas_call | solution.py:578

commit v6 on v5

--- a/solution.py
+++ b/solution.py
@@ -113,10 +113,14 @@
     back = (faces[1], faces[0], faces[3], faces[2])
 
     barrier = pltpu.get_barrier_semaphore()
-    greeted = list(faces)
-    greeted += [xc_peer(d) for d in range(1, nx * nc)]
-    greeted += [y_peer(d) for d in range(1, ny)]
-    greeted += [z_peer(d) for d in range(1, nz)]
+    def far_first(n):
+        return sorted(range(1, n), key=lambda d: -min(d, n - d))
+
+    greeted = []
+    for in_y, in_z in zip(far_first(ny), far_first(nz)):
+        greeted += [y_peer(in_y), z_peer(in_z)]
+    greeted = greeted[:6] + list(faces) + greeted[6:]
+    greeted += [xc_peer(d) for d in far_first(nx * nc)]
     for other in greeted:
         pl.semaphore_signal(
             barrier, inc=1, device_id=other, device_id_type=pl.DeviceIdType.MESH
@@ -148,9 +152,6 @@
         for copy in sent[len(settled) : upto]:
             copy.wait_send()
             settled.append(copy)
-
-    def far_first(n):
-        return sorted(range(1, n), key=lambda d: -min(d, n - d))
 
     def rows(ref, start, size):
         return ref.at[pl.ds(pl.multiple_of(start, 16), size)]
@@ -355,7 +356,7 @@
             rgx.at[d - 1],
             xc_peer(d),
         )
-        for d in range(1, nx * nc)
+        for d in far_first(nx * nc)
     ]
 
     ggout[...] = table_sum[A:, :].astype(BF)

time: 58.9 us -> 58.8 us (level)
  no operation moved by 1% of the time
where the time goes in v6:
time: 58.8 us; the launch traced here: 58.6 us
  Pallas kernels  57.3 us (97%)
  between operations  1.29 us (2%)
    pallas_call x1, Pallas kernels, local(): pl.pallas_call(kernel, out_shape=jax.ShapeDtypeStruct((7 * C, C), F32), i...  55.5 us
    pallas_call x1, Pallas kernels, local(): pl.pallas_call(place, out_shape=[jax.ShapeDtypeStruct((A, C), BF)] * 2 +...  1.83 us

profile of v6, /device:TPU:1, one launch (start us, length us, event | category | flops | bytes accessed | tf_op | source)
XLA Modules:
  0.0 58.6 jit_solution(16883370666687279135)
XLA Ops:
  1.3 55.5 %ewald_layer.1.rows = f32[896,128]{1,0:T(8,128)} custom-call(bf16[128,128]{1,0:T(8,128)(2,1)} %refs_0_.1, f32[3,128]{1,0:T(4,128)} %refs_1_.1, s32[64,128]{1,0:T(8,128)} %bitcast.5, f32[64,128]{1,0:T(8,128)} %bitcast.6, s32[4,32]{1,0:T(4,128)} %refs_4_.1, s32[1]{0:T(128)S(6)} %copy.23.refs_5_, f32[3,2048]{1,0:T(4,128)} %refs_6_.1, f32[1,2048]{1,0:T(1,128)} %bitcast.8, ...), custom_call_target="tpu_custom_call" | custom-call | tf_op jit(solution)/shard_map/ewald_layer/pallas_call | solution.py:568
  56.8 1.8 %place_outputs.1 = (bf16[128,128]{1,0:T(8,128)(2,1)}, bf16[128,128]{1,0:T(8,128)(2,1)}, f32[128,128]{1,0:T(8,128)}, f32[128,128]{1,0:T(8,128)}, f32[128,128]{1,0...) custom-call(f32[896,128]{1,0:T(8,128)} %ewald_layer.1.rows), custom_call_target="tpu_custom_call" | custom-call | tf_op jit(solution)/shard_map/place_outputs/pallas_call | solution.py:579
